TPU v7x, 512 devices: a whole 4x4x16 slice. The times are simulated.
512 devices in a mesh: ladder: 16 (over x, z_hi, core), space: 32 (over z_lo, y).
Axes of the slice: x: 4, y: 4, z: 16 (z_hi: 2, z_lo: 8; z = z_hi * 8 + z_lo), core: 2. Of those that a mesh axis runs over, the one named last changes fastest.
Arguments:
- initial: float32 [16, 1024, 2048], P('ladder', 'space'), may hold values from -1.2 to 1.2
- mobility: float32 [1024, 2048], P('space'), may hold values from 0.1 to 0.5
- tilt: float32 [1024, 2048], P('space'), may hold values from -0.5 to 0.5
- drift: float32 [2048], replicated, may hold values from -0.6 to 0.6
- mix_weights: float32 [16, 2], P('ladder'), may hold values from 0.2 to 0.4
Outputs:
- path: float32 [16, 1024, 2048], P('ladder', 'space')
All inputs are finite; a program needn't handle non-finite values.
Results may differ from a plain program's by a relative error of at most 0.00002.
Values sent between devices are 32-bit elements; how exact they have to be, the bound alone decides.
No kernel may reach another device: no remote copies, remote signals or barrier semaphores. Data moves between devices by JAX's collectives and lax.ppermute only.
A program may use at most 64 MiB of HBM per device.

v0:
```python
import jax
import jax.numpy as jnp
from jax import lax
from jax.sharding import PartitionSpec as P

CYCLES = 2


def with_halo(cells, sides, width, closed):
    for axis, dim in sides:
        count = lax.axis_size(axis)
        ends = count if closed else count - 1
        head = lax.slice_in_dim(cells, 0, width, axis=dim)
        tail = lax.slice_in_dim(cells, cells.shape[dim] - width, cells.shape[dim], axis=dim)
        cells = jnp.concatenate(
            [
                lax.ppermute(tail, axis, [(i, (i + 1) % count) for i in range(ends)]),
                cells,
                lax.ppermute(head, axis, [((i + 1) % count, i) for i in range(ends)]),
            ],
            axis=dim,
        )
    return cells


def advance(field, mobility, tilt, rising, falling):
    below = jnp.roll(field, 1, -2)
    above = jnp.roll(field, -1, -2)
    vertical = below + above
    horizontal = jnp.roll(field, 1, -1) + jnp.roll(field, -1, -1)
    laplace = vertical + horizontal - 4.0 * field
    transport = rising * (field - below) + falling * (above - field)
    return field + 0.1 * mobility * (laplace + field - field * field * field + tilt) - transport


def body(initial, mobility, tilt, drift, mix_weights):
    depth = 12
    height = initial.shape[1]
    coeffs = with_halo(jnp.stack([mobility, tilt]), (("space", 1),), depth, True)
    mob_rim = coeffs[0]
    tilt_rim = coeffs[1]
    rising = jnp.maximum(drift, 0.0)[None, :]
    falling = jnp.minimum(drift, 0.0)[None, :]
    field = initial[0]
    lower_w = mix_weights[0, 0]
    upper_w = mix_weights[0, 1]
    count = lax.axis_size("ladder")
    place = lax.axis_index("ladder")
    for cycle in range(CYCLES):
        extended = with_halo(field, (("space", 0),), depth, True)
        for inner in range(depth):
            extended = advance(extended, mob_rim, tilt_rim, rising, falling)
        field = extended[depth : depth + height]
        beside = with_halo(field[None], (("ladder", 0),), 1, False)
        lower = jnp.where(place == 0, field, beside[0])
        upper = jnp.where(place == count - 1, field, beside[2])
        field = (1.0 - lower_w - upper_w) * field + lower_w * lower + upper_w * upper
    return field[None]


def solution(mesh):
    in_specs = (
        P("ladder", "space", None),
        P("space", None),
        P("space", None),
        P(),
        P("ladder", None),
    )
    out_specs = P("ladder", "space", None)
    return jax.shard_map(body, mesh=mesh, in_specs=in_specs, out_specs=out_specs, check_vma=False)
```

profile of v0, /device:TPU:3, one launch (start us, length us, event | category | flops | bytes accessed | tf_op | source)
XLA Modules:
  0.0 132.3 jit_solution(4002728840718365109)
XLA Ops:
  0.0 1.2 fusion.199
  1.2 3.2 %collective-permute-start.2 = (f32[2,12,2048]{2,1,0:T(8,128)S(1)}, f32[2,12,2048]{2,1,0:T(8,128)S(1)}, u32[]{:S(2)}, u32[]{:S(2)}) collective-permute-start(f32[2,12,2048]{2,1,0:T(8,128)S(1)} %get-tuple-element.11), channel_id=1, source_target_pairs={{0,1},{1,2},{2,3},{3,4},{4,5},{5,6},{6,7},{7,8},{8,9},{9,10},{10,1... | collective-permute-start | bytes 589832 | tf_op jit(solution)/shard_map/ppermute | solution.py:17
  4.4 14.0 %collective-permute-start.3 = (f32[2,12,2048]{2,1,0:T(8,128)S(1)}, f32[2,12,2048]{2,1,0:T(8,128)S(1)}, u32[]{:S(2)}, u32[]{:S(2)}) collective-permute-start(f32[2,12,2048]{2,1,0:T(8,128)S(1)} %get-tuple-element.12), channel_id=1, source_target_pairs={{1,0},{2,1},{3,2},{4,3},{5,4},{6,5},{7,6},{8,7},{9,8},{10,9},{11,1... | collective-permute-start | bytes 589832 | tf_op jit(solution)/shard_map/ppermute | solution.py:19
  18.5 1.9 %collective-permute-start = (f32[12,2048]{1,0:T(8,128)S(1)}, f32[12,2048]{1,0:T(8,128)S(1)}, u32[]{:S(2)}, u32[]{:S(2)}) collective-permute-start(f32[12,2048]{1,0:T(8,128)S(1)} %get-tuple-element.203), channel_id=1, source_target_pairs={{0,1},{1,2},{2,3},{3,4},{4,5},{5,6},{6,7},{7,8},{8,9},{9,10},{10,1... | collective-permute-start | bytes 294920 | tf_op jit(solution)/shard_map/ppermute | solution.py:17
  20.4 12.1 %collective-permute-start.1 = (f32[12,2048]{1,0:T(8,128)S(1)}, f32[12,2048]{1,0:T(8,128)S(1)}, u32[]{:S(2)}, u32[]{:S(2)}) collective-permute-start(f32[12,2048]{1,0:T(8,128)S(1)} %get-tuple-element.204), channel_id=1, source_target_pairs={{1,0},{2,1},{3,2},{4,3},{5,4},{6,5},{7,6},{8,7},{9,8},{10,9},{11,1... | collective-permute-start | bytes 294920 | tf_op jit(solution)/shard_map/ppermute | solution.py:19
  32.9 1.5 %collective-permute-done.1 = f32[12,2048]{1,0:T(8,128)S(1)} collective-permute-done((f32[12,2048]{1,0:T(8,128)S(1)}, f32[12,2048]{1,0:T(8,128)S(1)}, u32[]{:S(2)}, u32[]{:S(2)}) %collective-permute-start.1) | collective-permute-done | bytes 98336 | tf_op jit(solution)/shard_map/ppermute | solution.py:19
  34.9 0.6 copy-done.1
  35.8 0.6 slice-done
  45.9 14.4 %collective-permute-start.4 = (f32[1,32,2048]{2,1,0:T(8,128)S(1)}, f32[1,32,2048]{2,1,0:T(8,128)S(1)}, u32[]{:S(2)}, u32[]{:S(2)}) collective-permute-start(f32[1,32,2048]{2,1,0:T(8,128)S(1)} %bitcast.145), channel_id=1, source_target_pairs={{0,32},{32,64},{64,96},{96,128},{128,160},{160,192},{192,224},{224... | collective-permute-start | bytes 786440 | tf_op jit(solution)/shard_map/ppermute | solution.py:17
  60.3 1.9 %collective-permute-start.5 = (f32[1,32,2048]{2,1,0:T(8,128)S(1)}, f32[1,32,2048]{2,1,0:T(8,128)S(1)}, u32[]{:S(2)}, u32[]{:S(2)}) collective-permute-start(f32[1,32,2048]{2,1,0:T(8,128)S(1)} %bitcast.146), channel_id=1, source_target_pairs={{32,0},{64,32},{96,64},{128,96},{160,128},{192,160},{224,192},{256... | collective-permute-start | bytes 786440 | tf_op jit(solution)/shard_map/ppermute | solution.py:19
  62.3 0.6 copy-done.7
  64.7 2.7 %collective-permute-done.4 = f32[1,32,2048]{2,1,0:T(8,128)S(1)} collective-permute-done((f32[1,32,2048]{2,1,0:T(8,128)S(1)}, f32[1,32,2048]{2,1,0:T(8,128)S(1)}, u32[]{:S(2)}, u32[]{:S(2)}) %collective-permute-start.4) | collective-permute-done | bytes 262176 | tf_op jit(solution)/shard_map/ppermute | solution.py:17
  67.4 10.6 %collective-permute-done.5 = f32[1,32,2048]{2,1,0:T(8,128)S(1)} collective-permute-done((f32[1,32,2048]{2,1,0:T(8,128)S(1)}, f32[1,32,2048]{2,1,0:T(8,128)S(1)}, u32[]{:S(2)}, u32[]{:S(2)}) %collective-permute-start.5) | collective-permute-done | bytes 262176 | tf_op jit(solution)/shard_map/ppermute | solution.py:19
  78.1 1.3 fusion.214
  79.4 1.9 %collective-permute-start.6 = (f32[12,2048]{1,0:T(8,128)S(1)}, f32[12,2048]{1,0:T(8,128)S(1)}, u32[]{:S(2)}, u32[]{:S(2)}) collective-permute-start(f32[12,2048]{1,0:T(8,128)S(1)} %get-tuple-element.201), channel_id=1, source_target_pairs={{0,1},{1,2},{2,3},{3,4},{4,5},{5,6},{6,7},{7,8},{8,9},{9,10},{10,1... | collective-permute-start | bytes 294920 | tf_op jit(solution)/shard_map/ppermute | solution.py:17
  81.3 12.3 %collective-permute-start.7 = (f32[12,2048]{1,0:T(8,128)S(1)}, f32[12,2048]{1,0:T(8,128)S(1)}, u32[]{:S(2)}, u32[]{:S(2)}) collective-permute-start(f32[12,2048]{1,0:T(8,128)S(1)} %get-tuple-element.202), channel_id=1, source_target_pairs={{1,0},{2,1},{3,2},{4,3},{5,4},{6,5},{7,6},{8,7},{9,8},{10,9},{11,1... | collective-permute-start | bytes 294920 | tf_op jit(solution)/shard_map/ppermute | solution.py:19
  93.8 1.5 %collective-permute-done.7 = f32[12,2048]{1,0:T(8,128)S(1)} collective-permute-done((f32[12,2048]{1,0:T(8,128)S(1)}, f32[12,2048]{1,0:T(8,128)S(1)}, u32[]{:S(2)}, u32[]{:S(2)}) %collective-permute-start.7) | collective-permute-done | bytes 98336 | tf_op jit(solution)/shard_map/ppermute | solution.py:19
  95.7 0.7 slice-done.1
  96.4 1.4 %fusion.65 = f32[56,2048]{1,0:T(8,128)S(1)} fusion(f32[56,2047]{1,0:T(8,128)S(1)} %get-tuple-element.104, f32[56,1]{1,0:T(8,128)S(1)} %get-tuple-element.106, f32[56,1]{1,0:T(8,128)S(1)} %get-tuple-element.105, f32[56,2047]{1,0:T(8,128)S(1)} %get-tuple-element.103, f32[1,2048]{1,0:T(1,128)S(1)} %slice-done.1, f32[55,2048]{1,0:T(8,128)S(1)} %get-tuple-element.102, ...), kind=kLoop, calls=%fused_computation.98 | loop fusion | flops 2867200 | bytes 3686400 | tf_op jit(solution)/shard_map/sub | solution.py:33
  106.7 4.0 %collective-permute-start.8 = (f32[1,32,2048]{2,1,0:T(8,128)S(1)}, f32[1,32,2048]{2,1,0:T(8,128)S(1)}, u32[]{:S(2)}, u32[]{:S(2)}) collective-permute-start(f32[1,32,2048]{2,1,0:T(8,128)S(1)} %bitcast.147), channel_id=1, source_target_pairs={{0,32},{32,64},{64,96},{96,128},{128,160},{160,192},{192,224},{224... | collective-permute-start | bytes 786440 | tf_op jit(solution)/shard_map/ppermute | solution.py:17
  110.8 1.9 %collective-permute-start.9 = (f32[1,32,2048]{2,1,0:T(8,128)S(1)}, f32[1,32,2048]{2,1,0:T(8,128)S(1)}, u32[]{:S(2)}, u32[]{:S(2)}) collective-permute-start(f32[1,32,2048]{2,1,0:T(8,128)S(1)} %bitcast.148), channel_id=1, source_target_pairs={{32,0},{64,32},{96,64},{128,96},{160,128},{192,160},{224,192},{256... | collective-permute-start | bytes 786440 | tf_op jit(solution)/shard_map/ppermute | solution.py:19
  112.7 11.0 %collective-permute-done.8 = f32[1,32,2048]{2,1,0:T(8,128)S(1)} collective-permute-done((f32[1,32,2048]{2,1,0:T(8,128)S(1)}, f32[1,32,2048]{2,1,0:T(8,128)S(1)}, u32[]{:S(2)}, u32[]{:S(2)}) %collective-permute-start.8) | collective-permute-done | bytes 262176 | tf_op jit(solution)/shard_map/ppermute | solution.py:17
  123.7 6.6 %collective-permute-done.9 = f32[1,32,2048]{2,1,0:T(8,128)S(1)} collective-permute-done((f32[1,32,2048]{2,1,0:T(8,128)S(1)}, f32[1,32,2048]{2,1,0:T(8,128)S(1)}, u32[]{:S(2)}, u32[]{:S(2)}) %collective-permute-start.9) | collective-permute-done | bytes 262176 | tf_op jit(solution)/shard_map/ppermute | solution.py:19
  130.3 2.0 %fusion.210 = f32[1,32,2048]{2,1,0:T(8,128)} fusion(f32[32,2048]{1,0:T(8,128)S(1)} %fusion.187, f32[1,32,2048]{2,1,0:T(8,128)S(1)} %collective-permute-done.9, f32[1,32,2048]{2,1,0:T(8,128)S(1)} %collective-permute-done.8, f32[]{:T(128)} %bitcast.1, f32[]{:T(128)} %bitcast, f32[]{:T(128)S(6)} %sub.369, pred[]{:T(512)S(6)} %eq.9, pred[]{:T(512)S(6)} %eq.8), kind=kLoop, calls=%fused_computation.325 | loop fusion | flops 458752 | bytes 1048590 | tf_op jit(solution)/shard_map/broadcast_in_dim | solution.py:58
  (149 shorter events, 20.4 us)
Async XLA Ops:
  0.0 18.4 %copy-start = (f32[1,32,2048]{2,1,0:T(8,128)S(1)}, f32[1,32,2048]{2,1,0:T(8,128)}, u32[]{:S(2)}) copy-start(f32[1,32,2048]{2,1,0:T(8,128)} %param.5) | copy-start | bytes 786436
  1.2 33.7 %collective-permute-start.2 = (f32[2,12,2048]{2,1,0:T(8,128)S(1)}, f32[2,12,2048]{2,1,0:T(8,128)S(1)}, u32[]{:S(2)}, u32[]{:S(2)}) collective-permute-start(f32[2,12,2048]{2,1,0:T(8,128)S(1)} %get-tuple-element.11), channel_id=1, source_target_pairs={{0,1},{1,2},{2,3},{3,4},{4,5},{5,6},{6,7},{7,8},{8,9},{9,10},{10,1... | collective-permute-start | bytes 589832 | tf_op jit(solution)/shard_map/ppermute | solution.py:17
  4.4 30.5 %collective-permute-start.3 = (f32[2,12,2048]{2,1,0:T(8,128)S(1)}, f32[2,12,2048]{2,1,0:T(8,128)S(1)}, u32[]{:S(2)}, u32[]{:S(2)}) collective-permute-start(f32[2,12,2048]{2,1,0:T(8,128)S(1)} %get-tuple-element.12), channel_id=1, source_target_pairs={{1,0},{2,1},{3,2},{4,3},{5,4},{6,5},{7,6},{8,7},{9,8},{10,9},{11,1... | collective-permute-start | bytes 589832 | tf_op jit(solution)/shard_map/ppermute | solution.py:19
  18.5 14.1 %copy-start.6 = (f32[2048]{0:T(1024)S(1)}, f32[2048]{0:T(1024)}, u32[]{:S(2)}) copy-start(f32[2048]{0:T(1024)} %param.8) | copy-start | bytes 24580
  18.5 14.4 %collective-permute-start = (f32[12,2048]{1,0:T(8,128)S(1)}, f32[12,2048]{1,0:T(8,128)S(1)}, u32[]{:S(2)}, u32[]{:S(2)}) collective-permute-start(f32[12,2048]{1,0:T(8,128)S(1)} %get-tuple-element.203), channel_id=1, source_target_pairs={{0,1},{1,2},{2,3},{3,4},{4,5},{5,6},{6,7},{7,8},{8,9},{9,10},{10,1... | collective-permute-start | bytes 294920 | tf_op jit(solution)/shard_map/ppermute | solution.py:17
  20.4 14.0 %collective-permute-start.1 = (f32[12,2048]{1,0:T(8,128)S(1)}, f32[12,2048]{1,0:T(8,128)S(1)}, u32[]{:S(2)}, u32[]{:S(2)}) collective-permute-start(f32[12,2048]{1,0:T(8,128)S(1)} %get-tuple-element.204), channel_id=1, source_target_pairs={{1,0},{2,1},{3,2},{4,3},{5,4},{6,5},{7,6},{8,7},{9,8},{10,9},{11,1... | collective-permute-start | bytes 294920 | tf_op jit(solution)/shard_map/ppermute | solution.py:19
  32.9 1.9 %copy-start.3 = (f32[12,2048]{1,0:T(8,128)}, f32[12,2048]{1,0:T(8,128)S(1)}, u32[]{:S(2)}) copy-start(f32[12,2048]{1,0:T(8,128)S(1)} %collective-permute-done) | copy-start | bytes 294916
  34.6 1.0 copy-start.1
  34.6 1.0 copy-start.2
  34.9 0.9 copy-start.4
  35.7 0.7 slice-start
  45.9 21.5 %collective-permute-start.4 = (f32[1,32,2048]{2,1,0:T(8,128)S(1)}, f32[1,32,2048]{2,1,0:T(8,128)S(1)}, u32[]{:S(2)}, u32[]{:S(2)}) collective-permute-start(f32[1,32,2048]{2,1,0:T(8,128)S(1)} %bitcast.145), channel_id=1, source_target_pairs={{0,32},{32,64},{64,96},{96,128},{128,160},{160,192},{192,224},{224... | collective-permute-start | bytes 786440 | tf_op jit(solution)/shard_map/ppermute | solution.py:17
  60.3 17.7 %collective-permute-start.5 = (f32[1,32,2048]{2,1,0:T(8,128)S(1)}, f32[1,32,2048]{2,1,0:T(8,128)S(1)}, u32[]{:S(2)}, u32[]{:S(2)}) collective-permute-start(f32[1,32,2048]{2,1,0:T(8,128)S(1)} %bitcast.146), channel_id=1, source_target_pairs={{32,0},{64,32},{96,64},{128,96},{160,128},{192,160},{224,192},{256... | collective-permute-start | bytes 786440 | tf_op jit(solution)/shard_map/ppermute | solution.py:19
  62.3 0.7 copy-start.7
  79.4 14.4 %collective-permute-start.6 = (f32[12,2048]{1,0:T(8,128)S(1)}, f32[12,2048]{1,0:T(8,128)S(1)}, u32[]{:S(2)}, u32[]{:S(2)}) collective-permute-start(f32[12,2048]{1,0:T(8,128)S(1)} %get-tuple-element.201), channel_id=1, source_target_pairs={{0,1},{1,2},{2,3},{3,4},{4,5},{5,6},{6,7},{7,8},{8,9},{9,10},{10,1... | collective-permute-start | bytes 294920 | tf_op jit(solution)/shard_map/ppermute | solution.py:17
  81.3 14.0 %collective-permute-start.7 = (f32[12,2048]{1,0:T(8,128)S(1)}, f32[12,2048]{1,0:T(8,128)S(1)}, u32[]{:S(2)}, u32[]{:S(2)}) collective-permute-start(f32[12,2048]{1,0:T(8,128)S(1)} %get-tuple-element.202), channel_id=1, source_target_pairs={{1,0},{2,1},{3,2},{4,3},{5,4},{6,5},{7,6},{8,7},{9,8},{10,9},{11,1... | collective-permute-start | bytes 294920 | tf_op jit(solution)/shard_map/ppermute | solution.py:19
  93.8 1.9 %copy-start.5 = (f32[12,2048]{1,0:T(8,128)}, f32[12,2048]{1,0:T(8,128)S(1)}, u32[]{:S(2)}) copy-start(f32[12,2048]{1,0:T(8,128)S(1)} %collective-permute-done.6) | copy-start | bytes 294916
  95.7 0.7 slice-start.1
  106.7 17.0 %collective-permute-start.8 = (f32[1,32,2048]{2,1,0:T(8,128)S(1)}, f32[1,32,2048]{2,1,0:T(8,128)S(1)}, u32[]{:S(2)}, u32[]{:S(2)}) collective-permute-start(f32[1,32,2048]{2,1,0:T(8,128)S(1)} %bitcast.147), channel_id=1, source_target_pairs={{0,32},{32,64},{64,96},{96,128},{128,160},{160,192},{192,224},{224... | collective-permute-start | bytes 786440 | tf_op jit(solution)/shard_map/ppermute | solution.py:17
  110.8 19.6 %collective-permute-start.9 = (f32[1,32,2048]{2,1,0:T(8,128)S(1)}, f32[1,32,2048]{2,1,0:T(8,128)S(1)}, u32[]{:S(2)}, u32[]{:S(2)}) collective-permute-start(f32[1,32,2048]{2,1,0:T(8,128)S(1)} %bitcast.148), channel_id=1, source_target_pairs={{32,0},{64,32},{96,64},{128,96},{160,128},{192,160},{224,192},{256... | collective-permute-start | bytes 786440 | tf_op jit(solution)/shard_map/ppermute | solution.py:19
where the time goes:
time: 133 us; the launch traced here: 132 us
  starting transfers between devices  67.7 us (51%)
  waiting for transfers between devices  34.7 us (26%)
  other arithmetic  16.5 us (12%)
  local copies, waits for them, and re-layouts  11.6 us (9%)
  between operations  1.89 us (1%)
    ppermute x5, starting transfers between devices, with_halo(): lax.ppermute(head, axis, [((i + 1) % count, i) for i in range(ends)])  42.2 us
    ppermute x5, starting transfers between devices, with_halo(): lax.ppermute(tail, axis, [(i, (i + 1) % count) for i in range(ends)])  25.5 us
    ppermute x5, waiting for transfers between devices, with_halo(): lax.ppermute(head, axis, [((i + 1) % count, i) for i in range(ends)])  20.3 us
    ppermute x5, waiting for transfers between devices, with_halo(): lax.ppermute(tail, axis, [(i, (i + 1) % count) for i in range(ends)])  14.4 us
    sub x22, other arithmetic, advance(): field + 0.1 * mobility * (laplace + field - field * field * field + tilt)  10.4 us
    slice x48, local copies, waits for them, and re-layouts, advance(): horizontal = jnp.roll(field, 1, -1) + jnp.roll(field, -1, -1)  6.24 us
  transfers between devices with their start and end apart: 10, of which 8 were waited for; matrix products, arithmetic and copies ran while one was open for 1% of the time, Pallas kernels for 0%

commit v1 on v0

v1 whole, which is shorter than its diff:
```python
import functools

import jax
import jax.numpy as jnp
from jax import lax
from jax.experimental import pallas as pl
from jax.experimental.pallas import tpu as pltpu
from jax.sharding import PartitionSpec as P

DEPTH = 12
RIM = 2 * DEPTH
LANES = 128
SUB = 8
FIRST = 36


def spans(k, cycle, height):
    rim = RIM - DEPTH * cycle
    begin = FIRST - rim + k
    end = FIRST + height + rim - k
    return begin // SUB, -(-end // SUB)


def sweep(src, dst, mob, tilt, drift, span):
    planes = src.shape[0]
    lane = lax.broadcasted_iota(jnp.int32, (SUB, LANES), 1)
    is_first = lane == 0
    is_last = lane == LANES - 1
    for j in range(planes):
        u = jnp.broadcast_to(drift[j : j + 1, :], (SUB, LANES))
        rising = u > 0
        speed = jnp.abs(u)
        left = (j - 1) % planes
        right = (j + 1) % planes
        for i in range(*span):
            r = i * SUB
            f = src[j, r : r + SUB, :]
            below = src[j, r - 1 : r - 1 + SUB, :]
            above = src[j, r + 1 : r + 1 + SUB, :]
            west = pltpu.roll(jnp.where(is_last, src[left, r : r + SUB, :], f), 1, 1)
            east = pltpu.roll(jnp.where(is_first, src[right, r : r + SUB, :], f), LANES - 1, 1)
            near = (west + east) + (below + above)
            m = mob[j, r : r + SUB, :]
            t = tilt[j, r : r + SUB, :]
            gain = m * ((near + t) - f * (f * f + 3.0))
            dst[j, r : r + SUB, :] = (f + gain) + speed * (jnp.where(rising, below, above) - f)


def run_cycle(a, b, mob, tilt, drift, cycle, height):
    k = 1
    while k <= DEPTH:
        span = spans(k, cycle, height)
        last = k
        while last < DEPTH and spans(last + 1, cycle, height) == span:
            last += 1
        if k % 2 == 0:
            sweep(b, a, mob, tilt, drift, span)
            k += 1
            continue
        pairs = (last - k + 1) // 2
        if pairs:

            @pl.loop(0, pairs)
            def _(_):
                sweep(a, b, mob, tilt, drift, span)
                sweep(b, a, mob, tilt, drift, span)

            k += 2 * pairs
        else:
            sweep(a, b, mob, tilt, drift, span)
            k += 1


def place(dst, at, ref):
    for j in range(dst.shape[0]):
        for r in range(0, ref.shape[0], SUB):
            dst[j, at + r : at + r + SUB, :] = ref[r : r + SUB, j * LANES : (j + 1) * LANES]


def blank(ref, height):
    lo = FIRST - RIM
    hi = FIRST + height + RIM
    planes, rows, _ = ref.shape
    for j in range(planes):
        ref[j, 0:16, :] = jnp.zeros((16, LANES), jnp.float32)
        ref[j, rows - 16 : rows, :] = jnp.zeros((16, LANES), jnp.float32)


def own_kernel(u, lo, hi, mb, tl, clo, chi, drift, p, mob, tilt, a, b):
    height = u.shape[0]
    planes = a.shape[0]
    for ref in (a, b, mob, tilt):
        blank(ref, height)
    for k, (dst, src, scale) in enumerate(((mob, mb, 0.1), (tilt, tl, None))):
        for at, part in ((FIRST - RIM, clo.at[k]), (FIRST, src), (FIRST + height, chi.at[k])):
            for j in range(planes):
                for r in range(0, part.shape[0], SUB):
                    v = part[r : r + SUB, j * LANES : (j + 1) * LANES]
                    dst[j, at + r : at + r + SUB, :] = v if scale is None else v * scale
    place(a, FIRST - RIM, lo)
    place(a, FIRST, u)
    place(a, FIRST + height, hi)
    run_cycle(a, b, mob, tilt, drift, 0, height)
    p[...] = a[:, FIRST - DEPTH : FIRST + height + DEPTH, :]


def recv_kernel(u, lo, hi, mob, tilt, drift, p, a, b):
    height = u.shape[0]
    for ref in (a, b):
        blank(ref, height)
    place(a, FIRST - RIM, lo)
    place(a, FIRST, u)
    place(a, FIRST + height, hi)
    run_cycle(a, b, mob, tilt, drift, 0, height)
    p[...] = a[:, FIRST - DEPTH : FIRST + height + DEPTH, :]


def second_kernel(w, mid, one, two, mob, tilt, drift, q, a, b):
    planes, height, _ = q.shape
    for ref in (a, b):
        blank(ref, height)
    for j in range(planes):
        for r in range(0, mid.shape[1], SUB):
            at = FIRST - DEPTH + r
            a[j, at : at + SUB, :] = (
                w[0] * mid[j, r : r + SUB, :] + w[1] * one[j, r : r + SUB, :] + w[2] * two[j, r : r + SUB, :]
            )
    run_cycle(a, b, mob, tilt, drift, 1, height)
    q[...] = a[:, FIRST : FIRST + height, :]


def last_kernel(w, mid, one, two, out):
    for j in range(mid.shape[0]):
        for r in range(0, mid.shape[1], SUB):
            out[r : r + SUB, j * LANES : (j + 1) * LANES] = (
                w[0] * mid[j, r : r + SUB, :] + w[1] * one[j, r : r + SUB, :] + w[2] * two[j, r : r + SUB, :]
            )


VMEM = pl.BlockSpec(memory_space=pltpu.VMEM)
SMEM = pl.BlockSpec(memory_space=pltpu.SMEM)


def call(kernel, name, specs, shapes, scratch, ops):
    out = [jax.ShapeDtypeStruct(s, jnp.float32) for s in shapes]
    single = len(out) == 1
    return pl.pallas_call(
        kernel,
        out_shape=out[0] if single else out,
        in_specs=specs,
        out_specs=VMEM if single else [VMEM] * len(out),
        scratch_shapes=[pltpu.VMEM(s, jnp.float32) for s in scratch],
        compiler_params=pltpu.CompilerParams(vmem_limit_bytes=6 * 2**20),
        cost_estimate=pl.CostEstimate(flops=ops, bytes_accessed=2**20, transcendentals=0),
        name=name,
    )


def body(initial, mobility, tilt, drift, mix_weights):
    ladder = lax.axis_size("ladder")
    space = lax.axis_size("space")
    image = lax.axis_index("ladder")
    slab = lax.axis_index("space")
    height, cols = initial.shape[1:]
    planes = cols // LANES
    rows = height + 2 * RIM + 24
    work = (planes, rows, LANES)

    def off(i):
        return (i - 1) % ladder if i % 2 == 0 else (i + 1) % ladder

    def beyond(i):
        return (i - 3) % ladder if i % 2 == 0 else (i + 3) % ladder

    swap_off = [(i, off(i)) for i in range(ladder)]
    swap_on = [(i, i ^ 1) for i in range(ladder)]
    swap_beyond = [(i, beyond(i)) for i in range(ladder)]
    both = ("ladder", "space")
    rise = [
        (i * space + s, i * space + s + 1 if s < space - 1 else off(i) * space)
        for i in range(ladder)
        for s in range(space)
    ]
    fall = [(b, a) for a, b in rise]

    own = initial[0]
    other = lax.ppermute(own, "ladder", swap_off)
    coeffs = jnp.stack([mobility, tilt])
    c_lo = lax.ppermute(coeffs[:, height - RIM :], both, rise)
    c_hi = lax.ppermute(coeffs[:, :RIM], both, fall)
    own_lo = lax.ppermute(own[height - RIM :], "space", [(s, (s + 1) % space) for s in range(space)])
    own_hi = lax.ppermute(own[:RIM], "space", [((s + 1) % space, s) for s in range(space)])
    w_off = lax.ppermute(mix_weights, "ladder", swap_off)
    own_lo, w_off = lax.optimization_barrier((own_lo, w_off))
    w_off = w_off[0]
    w_own = mix_weights[0]
    flow = drift.reshape(planes, LANES)

    p_own, mob, til = call(
        own_kernel, "own_first", [VMEM] * 8, [(planes, height + 2 * DEPTH, LANES), work, work], [work, work], 10**8
    )(own, own_lo, own_hi, mobility, tilt, c_lo, c_hi, flow)
    p_on = lax.ppermute(p_own, "ladder", swap_on)

    top = jnp.where(slab == space - 1, own[height - RIM :], other[height - RIM :])
    bottom = jnp.where(slab == 0, own[:RIM], other[:RIM])
    off_lo = lax.ppermute(top, both, rise)
    off_hi = lax.ppermute(bottom, both, fall)
    p_off = call(
        recv_kernel, "off_first", [VMEM] * 6, [(planes, height + 2 * DEPTH, LANES)], [work, work], 10**8
    )(other, off_lo, off_hi, mob, til, flow)
    p_beyond = lax.ppermute(p_off, "ladder", swap_beyond)

    even = image % 2 == 0
    toward_off = jnp.where(even, w_own[0], w_own[1])
    toward_on = jnp.where(even, w_own[1], w_own[0])
    rest = 1.0 - w_own[0] - w_own[1]
    at_end = (image == 0) | (image == ladder - 1)
    w_mine = jnp.stack([jnp.where(at_end, rest + toward_off, rest), jnp.where(at_end, 0.0, toward_off), toward_on])
    back = jnp.where(even, w_off[1], w_off[0])
    on = jnp.where(even, w_off[0], w_off[1])
    w_theirs = jnp.stack([1.0 - w_off[0] - w_off[1], back, on])

    second = call(
        second_kernel, "second", [SMEM] + [VMEM] * 6, [(planes, height, LANES)], [work, work], 10**8
    )
    q_own = second(w_mine, p_own, p_off, p_on, mob, til, flow)
    q_on = lax.ppermute(q_own, "ladder", swap_on)
    q_off = second(w_theirs, p_off, p_own, p_beyond, mob, til, flow)
    path = call(last_kernel, "blend", [SMEM] + [VMEM] * 3, [(height, cols)], [], 10**6)(w_mine, q_own, q_off, q_on)
    return path[None]


def solution(mesh):
    in_specs = (
        P("ladder", "space", None),
        P("space", None),
        P("space", None),
        P(),
        P("ladder", None),
    )
    out_specs = P("ladder", "space", None)
    return jax.shard_map(body, mesh=mesh, in_specs=in_specs, out_specs=out_specs, check_vma=False)
```

time: 133 us -> 128 us (0.962)
  the two profiles are of different devices: /device:TPU:3 before, /device:TPU:1 now
where the time goes in v1:
time: 128 us; the launch traced here: 127 us
  starting transfers between devices  63.9 us (50%)
  waiting for transfers between devices  23.8 us (19%)
  Pallas kernels  19.1 us (15%)
  local copies, waits for them, and re-layouts  10.2 us (8%)
  between operations  7.79 us (6%)
  other arithmetic  2.17 us (2%)
    ppermute x1, waiting for transfers between devices, body(): w_off = lax.ppermute(mix_weights, 'ladder', swap_off)  18.5 us
    ppermute x1, starting transfers between devices, body(): c_hi = lax.ppermute(coeffs[:, :RIM], both, fall)  12.8 us
    ppermute x1, starting transfers between devices, body(): lax.ppermute(own[:RIM], 'space', [((s + 1) % space, s) for s in range(spa...  9.61 us
    ppermute x1, starting transfers between devices, body(): other = lax.ppermute(own, 'ladder', swap_off)  8.96 us
    unnamed x30, local copies, waits for them, and re-layouts  8.34 us
    ppermute x1, starting transfers between devices, body(): off_hi = lax.ppermute(bottom, both, fall)  6.96 us
    ppermute x1, starting transfers between devices, body(): p_on = lax.ppermute(p_own, 'ladder', swap_on)  5.96 us
    ppermute x1, starting transfers between devices, body(): w_off = lax.ppermute(mix_weights, 'ladder', swap_off)  5.44 us
  transfers between devices with their start and end apart: 11, of which 3 were waited for; matrix products, arithmetic and copies ran while one was open for 2% of the time, Pallas kernels for 14%

profile of v1, /device:TPU:1, one launch (start us, length us, event | category | flops | bytes accessed | tf_op | source)
XLA Modules:
  0.0 127.0 jit_solution(8027833332617060637)
XLA Ops:
  0.0 1.3 %pad_maximum_fusion = (f32[2,24,2048]{2,1,0:T(8,128)S(1)}, f32[2,24,2048]{2,1,0:T(8,128)S(1)}) fusion(f32[1,32,2048]{2,1,0:T(8,128)} %bitcast.26, f32[1,32,2048]{2,1,0:T(8,128)} %bitcast.25), kind=kLoop, calls=%fused_computation.3 | loop fusion | flops 196608 | bytes 1310720 | tf_op jit(solution)/shard_map/stack | solution.py:188
  1.3 4.0 %collective-permute-start.3 = (f32[2,24,2048]{2,1,0:T(8,128)S(1)}, f32[2,24,2048]{2,1,0:T(8,128)S(1)}, u32[]{:S(2)}, u32[]{:S(2)}) collective-permute-start(f32[2,24,2048]{2,1,0:T(8,128)S(1)} %get-tuple-element.18), channel_id=1, source_target_pairs={{0,1},{1,2},{2,3},{3,4},{4,5},{5,6},{6,7},{7,8},{8,9},{9,10},{10,1... | collective-permute-start | bytes 1179656 | tf_op jit(solution)/shard_map/ppermute | solution.py:189
  5.4 12.8 %collective-permute-start.4 = (f32[2,24,2048]{2,1,0:T(8,128)S(1)}, f32[2,24,2048]{2,1,0:T(8,128)S(1)}, u32[]{:S(2)}, u32[]{:S(2)}) collective-permute-start(f32[2,24,2048]{2,1,0:T(8,128)S(1)} %get-tuple-element.17), channel_id=1, source_target_pairs={{1,0},{2,1},{3,2},{4,3},{5,4},{6,5},{7,6},{8,7},{9,8},{10,9},{11,1... | collective-permute-start | bytes 1179656 | tf_op jit(solution)/shard_map/ppermute | solution.py:190
  18.2 9.0 %collective-permute-start.5 = (f32[32,2048]{1,0:T(8,128)S(1)}, f32[32,2048]{1,0:T(8,128)S(1)}, u32[]{:S(2)}, u32[]{:S(2)}) collective-permute-start(f32[32,2048]{1,0:T(8,128)S(1)} %bitcast.23), channel_id=1, source_target_pairs={{0,480},{32,64},{64,32},{96,128},{128,96},{160,192},{192,160},{224... | collective-permute-start | bytes 786440 | tf_op jit(solution)/shard_map/ppermute | solution.py:187
  27.9 2.0 %collective-permute-start = (f32[24,2048]{1,0:T(8,128)}, f32[24,2048]{1,0:T(8,128)S(1)}, u32[]{:S(2)}, u32[]{:S(2)}) collective-permute-start(f32[24,2048]{1,0:T(8,128)} %get-tuple-element.20), channel_id=1, source_target_pairs={{0,1},{1,2},{2,3},{3,4},{4,5},{5,6},{6,7},{7,8},{8,9},{9,10},{10,1... | collective-permute-start | bytes 589832 | tf_op jit(solution)/shard_map/ppermute | solution.py:191
  30.0 5.4 %collective-permute-start.1 = (f32[1,2]{1,0:T(1,128)S(1)}, f32[1,2]{1,0:T(1,128)S(1)}, u32[]{:S(2)}, u32[]{:S(2)}) collective-permute-start(f32[1,2]{1,0:T(1,128)S(1)} %copy-done.14), channel_id=1, source_target_pairs={{0,480},{32,64},{64,32},{96,128},{128,96},{160,192},{192,160},{224... | collective-permute-start | bytes 32 | tf_op jit(solution)/shard_map/ppermute | solution.py:193
  35.4 18.5 %collective-permute-done.1 = f32[1,2]{1,0:T(1,128)S(1)} collective-permute-done((f32[1,2]{1,0:T(1,128)S(1)}, f32[1,2]{1,0:T(1,128)S(1)}, u32[]{:S(2)}, u32[]{:S(2)}) %collective-permute-start.1) | collective-permute-done | bytes 40 | tf_op jit(solution)/shard_map/ppermute | solution.py:193
  54.0 9.6 %collective-permute-start.2 = (f32[24,2048]{1,0:T(8,128)S(1)}, f32[24,2048]{1,0:T(8,128)S(1)}, u32[]{:S(2)}, u32[]{:S(2)}) collective-permute-start(f32[24,2048]{1,0:T(8,128)S(1)} %get-tuple-element.19), channel_id=1, source_target_pairs={{1,0},{2,1},{3,2},{4,3},{5,4},{6,5},{7,6},{8,7},{9,8},{10,9},{11,1... | collective-permute-start | bytes 589832 | tf_op jit(solution)/shard_map/ppermute | solution.py:192
  64.3 1.9 %collective-permute-done.2.hi = f32[24,2048]{1,0:T(8,128)S(1)} collective-permute-done((f32[24,2048]{1,0:T(8,128)S(1)}, f32[24,2048]{1,0:T(8,128)S(1)}, u32[]{:S(2)}, u32[]{:S(2)}) %collective-permute-start.2) | collective-permute-done | bytes 196640 | tf_op jit(solution)/shard_map/ppermute | solution.py:192
  68.4 1.0 copy-done.4
  69.4 1.0 copy-done.6
  70.4 0.9 copy-done.10
  71.3 0.9 copy-done.12
  72.2 4.7 %own_first.1 = (f32[16,56,128]{2,1,0:T(8,128)S(1)}, f32[16,104,128]{2,1,0:T(8,128)S(1)}, f32[16,104,128]{2,1,0:T(8,128)S(1)}) custom-call(f32[32,2048]{1,0:T(8,128)S(1)} %bitcast.24, f32[24,2048]{1,0:T(8,128)S(1)} %copy-done.10, f32[24,2048]{1,0:T(8,128)S(1)} %copy-done.12, f32[32,2048]{1,0:T(8,128)S(1)} %copy-done.1, f32[32,2048]{1,0:T(8,128)S(1)} %copy-done.2, ...), custom_call_target="tpu_custom_call" | custom-call | flops 100000000 | bytes 1048576 | tf_op jit(solution)/shard_map/own_first/pallas_call | solution.py:199
  77.0 6.0 %collective-permute-start.8 = (f32[16,56,128]{2,1,0:T(8,128)S(1)}, f32[16,56,128]{2,1,0:T(8,128)S(1)}, u32[]{:S(2)}, u32[]{:S(2)}) collective-permute-start(f32[16,56,128]{2,1,0:T(8,128)S(1)} %get-tuple-element.11.mid.one), channel_id=1, source_target_pairs={{0,32},{32,0},{64,96},{96,64},{128,160},{160,128},{192,224},{224,1... | collective-permute-start | bytes 1376264 | tf_op jit(solution)/shard_map/ppermute | solution.py:202
  83.7 1.9 %collective-permute-start.6 = (f32[24,2048]{1,0:T(8,128)}, f32[24,2048]{1,0:T(8,128)S(1)}, u32[]{:S(2)}, u32[]{:S(2)}) collective-permute-start(f32[24,2048]{1,0:T(8,128)} %get-tuple-element.16), channel_id=1, source_target_pairs={{0,1},{1,2},{2,3},{3,4},{4,5},{5,6},{6,7},{7,8},{8,9},{9,10},{10,1... | collective-permute-start | bytes 589832 | tf_op jit(solution)/shard_map/ppermute | solution.py:206
  85.6 7.0 %collective-permute-start.7 = (f32[24,2048]{1,0:T(8,128)S(1)}, f32[24,2048]{1,0:T(8,128)S(1)}, u32[]{:S(2)}, u32[]{:S(2)}) collective-permute-start(f32[24,2048]{1,0:T(8,128)S(1)} %get-tuple-element.15), channel_id=1, source_target_pairs={{1,0},{2,1},{3,2},{4,3},{5,4},{6,5},{7,6},{8,7},{9,8},{10,9},{11,1... | collective-permute-start | bytes 589832 | tf_op jit(solution)/shard_map/ppermute | solution.py:207
  92.6 3.4 %collective-permute-done.6.lo = f32[24,2048]{1,0:T(8,128)S(1)} collective-permute-done((f32[24,2048]{1,0:T(8,128)}, f32[24,2048]{1,0:T(8,128)S(1)}, u32[]{:S(2)}, u32[]{:S(2)}) %collective-permute-start.6) | collective-permute-done | bytes 196640 | tf_op jit(solution)/shard_map/ppermute | solution.py:206
  97.6 4.6 %off_first.1.one.mid = f32[16,56,128]{2,1,0:T(8,128)S(1)} custom-call(f32[32,2048]{1,0:T(8,128)S(1)} %collective-permute-done.5.u, f32[24,2048]{1,0:T(8,128)S(1)} %collective-permute-done.6.lo, f32[24,2048]{1,0:T(8,128)S(1)} %copy-done.8, f32[16,104,128]{2,1,0:T(8,128)S(1)} %get-tuple-element.12.mob, f32[16,104,128]{2,1,0:T(8,128)S(1)} %get-tuple-element.13.tilt, ...), custom_call_target="tpu_custom_call" | custom-call | flops 100000000 | bytes 1048576 | tf_op jit(solution)/shard_map/off_first/pallas_call | solution.py:208
  102.2 4.2 %collective-permute-start.9 = (f32[16,56,128]{2,1,0:T(8,128)S(1)}, f32[16,56,128]{2,1,0:T(8,128)}, u32[]{:S(2)}, u32[]{:S(2)}) collective-permute-start(f32[16,56,128]{2,1,0:T(8,128)S(1)} %off_first.1.one.mid), channel_id=1, source_target_pairs={{0,416},{32,128},{64,480},{96,192},{128,32},{160,256},{192,96},{22... | collective-permute-start | bytes 1376264 | tf_op jit(solution)/shard_map/ppermute | solution.py:211
  110.7 4.0 %second.2.mid = f32[16,32,128]{2,1,0:T(8,128)S(1)} custom-call(f32[3]{0:T(128)S(1)} %pad_maximum_fusion.1.w, f32[16,56,128]{2,1,0:T(8,128)S(1)} %get-tuple-element.11.mid.one, f32[16,56,128]{2,1,0:T(8,128)S(1)} %off_first.1.one.mid, f32[16,56,128]{2,1,0:T(8,128)S(1)} %collective-permute-done.8.two, f32[16,104,128]{2,1,0:T(8,128)S(1)} %get-tuple-element.12.mob, ...), custom_call_target="tpu_custom_call" | custom-call | flops 100000000 | bytes 1048576 | tf_op jit(solution)/shard_map/second/pallas_call | solution.py:226
  114.7 1.9 %collective-permute-start.10 = (f32[16,32,128]{2,1,0:T(8,128)S(1)}, f32[16,32,128]{2,1,0:T(8,128)S(1)}, u32[]{:S(2)}, u32[]{:S(2)}) collective-permute-start(f32[16,32,128]{2,1,0:T(8,128)S(1)} %second.2.mid), channel_id=1, source_target_pairs={{0,32},{32,0},{64,96},{96,64},{128,160},{160,128},{192,224},{224,1... | collective-permute-start | bytes 786440 | tf_op jit(solution)/shard_map/ppermute | solution.py:227
  121.2 4.5 %second.3.one = f32[16,32,128]{2,1,0:T(8,128)S(1)} custom-call(f32[3]{0:T(128)S(1)} %pad_maximum_fusion.2.w, f32[16,56,128]{2,1,0:T(8,128)S(1)} %off_first.1.one.mid, f32[16,56,128]{2,1,0:T(8,128)S(1)} %get-tuple-element.11.mid.one, f32[16,56,128]{2,1,0:T(8,128)} %collective-permute-done.9.two, f32[16,104,128]{2,1,0:T(8,128)S(1)} %get-tuple-element.12.mob, ...), custom_call_target="tpu_custom_call" | custom-call | flops 100000000 | bytes 1048576 | tf_op jit(solution)/shard_map/second/pallas_call | solution.py:228
  125.7 1.3 %blend.1 = f32[32,2048]{1,0:T(8,128)} custom-call(f32[3]{0:T(128)S(1)} %pad_maximum_fusion.1.w, f32[16,32,128]{2,1,0:T(8,128)S(1)} %second.2.mid, f32[16,32,128]{2,1,0:T(8,128)S(1)} %second.3.one, f32[16,32,128]{2,1,0:T(8,128)S(1)} %collective-permute-done.10.two), custom_call_target="tpu_custom_call" | custom-call | flops 1000000 | bytes 1048576 | tf_op jit(solution)/shard_map/blend/pallas_call | solution.py:229
  (40 shorter events, 7.2 us)
Async XLA Ops:
  0.0 18.2 %copy-start = (f32[1,32,2048]{2,1,0:T(8,128)S(1)}, f32[1,32,2048]{2,1,0:T(8,128)}, u32[]{:S(2)}) copy-start(f32[1,32,2048]{2,1,0:T(8,128)} %param.5) | copy-start | bytes 786436
  1.3 65.6 %collective-permute-start.3 = (f32[2,24,2048]{2,1,0:T(8,128)S(1)}, f32[2,24,2048]{2,1,0:T(8,128)S(1)}, u32[]{:S(2)}, u32[]{:S(2)}) collective-permute-start(f32[2,24,2048]{2,1,0:T(8,128)S(1)} %get-tuple-element.18), channel_id=1, source_target_pairs={{0,1},{1,2},{2,3},{3,4},{4,5},{5,6},{6,7},{7,8},{8,9},{9,10},{10,1... | collective-permute-start | bytes 1179656 | tf_op jit(solution)/shard_map/ppermute | solution.py:189
  5.4 62.3 %collective-permute-start.4 = (f32[2,24,2048]{2,1,0:T(8,128)S(1)}, f32[2,24,2048]{2,1,0:T(8,128)S(1)}, u32[]{:S(2)}, u32[]{:S(2)}) collective-permute-start(f32[2,24,2048]{2,1,0:T(8,128)S(1)} %get-tuple-element.17), channel_id=1, source_target_pairs={{1,0},{2,1},{3,2},{4,3},{5,4},{6,5},{7,6},{8,7},{9,8},{10,9},{11,1... | collective-permute-start | bytes 1179656 | tf_op jit(solution)/shard_map/ppermute | solution.py:190
  18.2 50.2 %copy-start.1 = (f32[32,2048]{1,0:T(8,128)S(1)}, f32[32,2048]{1,0:T(8,128)}, u32[]{:S(2)}) copy-start(f32[32,2048]{1,0:T(8,128)} %mb.1) | copy-start | bytes 786436
  18.2 50.2 %copy-start.2 = (f32[32,2048]{1,0:T(8,128)S(1)}, f32[32,2048]{1,0:T(8,128)}, u32[]{:S(2)}) copy-start(f32[32,2048]{1,0:T(8,128)} %tl.1) | copy-start | bytes 786436
  18.2 64.7 %collective-permute-start.5 = (f32[32,2048]{1,0:T(8,128)S(1)}, f32[32,2048]{1,0:T(8,128)S(1)}, u32[]{:S(2)}, u32[]{:S(2)}) collective-permute-start(f32[32,2048]{1,0:T(8,128)S(1)} %bitcast.23), channel_id=1, source_target_pairs={{0,480},{32,64},{64,32},{96,128},{128,96},{160,192},{192,160},{224... | collective-permute-start | bytes 786440 | tf_op jit(solution)/shard_map/ppermute | solution.py:187
  27.2 2.8 %copy-start.14 = (f32[1,2]{1,0:T(1,128)S(1)}, f32[1,2]{1,0:T(1,128)}, u32[]{:S(2)}) copy-start(f32[1,2]{1,0:T(1,128)} %param.9) | copy-start | bytes 28
  27.9 40.5 %copy-start.13 = (f32[2048]{0:T(1024)S(1)}, f32[2048]{0:T(1024)}, u32[]{:S(2)}) copy-start(f32[2048]{0:T(1024)} %param.8) | copy-start | bytes 24580
  27.9 35.7 %collective-permute-start = (f32[24,2048]{1,0:T(8,128)}, f32[24,2048]{1,0:T(8,128)S(1)}, u32[]{:S(2)}, u32[]{:S(2)}) collective-permute-start(f32[24,2048]{1,0:T(8,128)} %get-tuple-element.20), channel_id=1, source_target_pairs={{0,1},{1,2},{2,3},{3,4},{4,5},{5,6},{6,7},{7,8},{8,9},{9,10},{10,1... | collective-permute-start | bytes 589832 | tf_op jit(solution)/shard_map/ppermute | solution.py:191
  30.0 24.0 %collective-permute-start.1 = (f32[1,2]{1,0:T(1,128)S(1)}, f32[1,2]{1,0:T(1,128)S(1)}, u32[]{:S(2)}, u32[]{:S(2)}) collective-permute-start(f32[1,2]{1,0:T(1,128)S(1)} %copy-done.14), channel_id=1, source_target_pairs={{0,480},{32,64},{64,32},{96,128},{128,96},{160,192},{192,160},{224... | collective-permute-start | bytes 32 | tf_op jit(solution)/shard_map/ppermute | solution.py:193
  54.0 12.2 %collective-permute-start.2 = (f32[24,2048]{1,0:T(8,128)S(1)}, f32[24,2048]{1,0:T(8,128)S(1)}, u32[]{:S(2)}, u32[]{:S(2)}) collective-permute-start(f32[24,2048]{1,0:T(8,128)S(1)} %get-tuple-element.19), channel_id=1, source_target_pairs={{1,0},{2,1},{3,2},{4,3},{5,4},{6,5},{7,6},{8,7},{9,8},{10,9},{11,1... | collective-permute-start | bytes 589832 | tf_op jit(solution)/shard_map/ppermute | solution.py:192
  66.2 0.7 copy-start.11
  66.9 0.8 copy-start.3
  67.6 0.8 copy-start.5
  68.4 1.0 copy-start.4
  69.4 1.0 copy-start.6
  70.4 0.9 copy-start.10
  71.3 0.9 copy-start.12
  77.0 33.7 %collective-permute-start.8 = (f32[16,56,128]{2,1,0:T(8,128)S(1)}, f32[16,56,128]{2,1,0:T(8,128)S(1)}, u32[]{:S(2)}, u32[]{:S(2)}) collective-permute-start(f32[16,56,128]{2,1,0:T(8,128)S(1)} %get-tuple-element.11.mid.one), channel_id=1, source_target_pairs={{0,32},{32,0},{64,96},{96,64},{128,160},{160,128},{192,224},{224,1... | collective-permute-start | bytes 1376264 | tf_op jit(solution)/shard_map/ppermute | solution.py:202
  83.7 12.3 %collective-permute-start.6 = (f32[24,2048]{1,0:T(8,128)}, f32[24,2048]{1,0:T(8,128)S(1)}, u32[]{:S(2)}, u32[]{:S(2)}) collective-permute-start(f32[24,2048]{1,0:T(8,128)} %get-tuple-element.16), channel_id=1, source_target_pairs={{0,1},{1,2},{2,3},{3,4},{4,5},{5,6},{6,7},{7,8},{8,9},{9,10},{10,1... | collective-permute-start | bytes 589832 | tf_op jit(solution)/shard_map/ppermute | solution.py:206
  85.6 10.4 %collective-permute-start.7 = (f32[24,2048]{1,0:T(8,128)S(1)}, f32[24,2048]{1,0:T(8,128)S(1)}, u32[]{:S(2)}, u32[]{:S(2)}) collective-permute-start(f32[24,2048]{1,0:T(8,128)S(1)} %get-tuple-element.15), channel_id=1, source_target_pairs={{1,0},{2,1},{3,2},{4,3},{5,4},{6,5},{7,6},{8,7},{9,8},{10,9},{11,1... | collective-permute-start | bytes 589832 | tf_op jit(solution)/shard_map/ppermute | solution.py:207
  96.6 0.9 copy-start.8
  102.2 19.0 %collective-permute-start.9 = (f32[16,56,128]{2,1,0:T(8,128)S(1)}, f32[16,56,128]{2,1,0:T(8,128)}, u32[]{:S(2)}, u32[]{:S(2)}) collective-permute-start(f32[16,56,128]{2,1,0:T(8,128)S(1)} %off_first.1.one.mid), channel_id=1, source_target_pairs={{0,416},{32,128},{64,480},{96,192},{128,32},{160,256},{192,96},{22... | collective-permute-start | bytes 1376264 | tf_op jit(solution)/shard_map/ppermute | solution.py:211
  114.7 11.0 %collective-permute-start.10 = (f32[16,32,128]{2,1,0:T(8,128)S(1)}, f32[16,32,128]{2,1,0:T(8,128)S(1)}, u32[]{:S(2)}, u32[]{:S(2)}) collective-permute-start(f32[16,32,128]{2,1,0:T(8,128)S(1)} %second.2.mid), channel_id=1, source_target_pairs={{0,32},{32,0},{64,96},{96,64},{128,160},{160,128},{192,224},{224,1... | collective-permute-start | bytes 786440 | tf_op jit(solution)/shard_map/ppermute | solution.py:227
  (2 other events, 1.4 us)

commit v2 on v1

v2 whole, which is shorter than its diff:
```python
import functools

import jax
import jax.numpy as jnp
from jax import lax
from jax.experimental import pallas as pl
from jax.experimental.pallas import tpu as pltpu
from jax.sharding import PartitionSpec as P

DEPTH = 12
RIM = 2 * DEPTH
LANES = 128
SUB = 8
FIRST = 36


def spans(k, cycle, height):
    rim = RIM - DEPTH * cycle
    begin = FIRST - rim + k
    end = FIRST + height + rim - k
    return begin // SUB, -(-end // SUB)


def sweep(src, dst, mob, tilt, drift, span):
    planes = src.shape[0]
    lane = lax.broadcasted_iota(jnp.int32, (SUB, LANES), 1)
    is_first = lane == 0
    is_last = lane == LANES - 1
    for j in range(planes):
        u = jnp.broadcast_to(drift[j : j + 1, :], (SUB, LANES))
        rising = u > 0
        speed = jnp.abs(u)
        left = (j - 1) % planes
        right = (j + 1) % planes
        for i in range(*span):
            r = i * SUB
            f = src[j, r : r + SUB, :]
            below = src[j, r - 1 : r - 1 + SUB, :]
            above = src[j, r + 1 : r + 1 + SUB, :]
            west = pltpu.roll(jnp.where(is_last, src[left, r : r + SUB, :], f), 1, 1)
            east = pltpu.roll(jnp.where(is_first, src[right, r : r + SUB, :], f), LANES - 1, 1)
            near = (west + east) + (below + above)
            m = mob[j, r : r + SUB, :]
            t = tilt[j, r : r + SUB, :]
            gain = m * ((near + t) - f * (f * f + 3.0))
            dst[j, r : r + SUB, :] = (f + gain) + speed * (jnp.where(rising, below, above) - f)


def run_cycle(a, b, mob, tilt, drift, cycle, height):
    k = 1
    while k <= DEPTH:
        span = spans(k, cycle, height)
        last = k
        while last < DEPTH and spans(last + 1, cycle, height) == span:
            last += 1
        if k % 2 == 0:
            sweep(b, a, mob, tilt, drift, span)
            k += 1
            continue
        pairs = (last - k + 1) // 2
        if pairs:

            @pl.loop(0, pairs)
            def _(_):
                sweep(a, b, mob, tilt, drift, span)
                sweep(b, a, mob, tilt, drift, span)

            k += 2 * pairs
        else:
            sweep(a, b, mob, tilt, drift, span)
            k += 1


def place(dst, at, tiles, first, count):
    planes = dst.shape[0]
    for j in range(planes):
        for i in range(count):
            r = at + i * SUB
            dst[j, r : r + SUB, :] = tiles[(first + i) * planes + j]


def blank(ref):
    planes, rows, _ = ref.shape
    for j in range(planes):
        ref[j, 0:16, :] = jnp.zeros((16, LANES), jnp.float32)
        ref[j, rows - 16 : rows, :] = jnp.zeros((16, LANES), jnp.float32)


def edges_kernel(msg, mobility, tilt, up, down, wrap):
    low_end = lax.axis_index("space") == 0
    planes = mobility.shape[1] // LANES
    tiles = mobility.shape[0] // SUB
    count = RIM // SUB
    skip = tiles - count
    for i in range(count):
        for j in range(planes):
            k = i * planes + j
            top = msg[k + skip * planes]
            bottom = msg[k]
            wrap[k] = jnp.where(low_end, bottom, top)
            lanes = slice(j * LANES, (j + 1) * LANES)
            lo = slice(i * SUB, (i + 1) * SUB)
            hi = slice((i + skip) * SUB, (i + skip + 1) * SUB)
            up[0, k] = top
            up[1, k] = mobility[hi, lanes]
            up[2, k] = tilt[hi, lanes]
            down[0, k] = bottom
            down[1, k] = mobility[lo, lanes]
            down[2, k] = tilt[lo, lanes]


def off_edges_kernel(msg, other, up, down):
    slab = lax.axis_index("space")
    low_end = slab == 0
    high_end = slab == lax.axis_size("space") - 1
    count = up.shape[0]
    skip = other.shape[0] - 1 - count
    for k in range(count):
        up[k] = jnp.where(high_end, msg[k + skip], other[k + skip])
        down[k] = jnp.where(low_end, msg[k], other[k])


def own_kernel(msg, lo, hi, wrap, mobility, tilt, drift, p, mob, til, a, b):
    slab = lax.axis_index("space")
    low_end = slab == 0
    high_end = slab == lax.axis_size("space") - 1
    height = mobility.shape[0]
    planes = a.shape[0]
    count = RIM // SUB
    for ref in (a, b, mob, til):
        blank(ref)
    for j in range(planes):
        for i in range(count):
            k = i * planes + j
            for at, got in ((FIRST - RIM, lo), (FIRST + height, hi)):
                r = at + i * SUB
                mob[j, r : r + SUB, :] = 0.1 * got[1, k]
                til[j, r : r + SUB, :] = got[2, k]
            r = FIRST - RIM + i * SUB
            a[j, r : r + SUB, :] = jnp.where(low_end, wrap[k], lo[0, k])
            r = FIRST + height + i * SUB
            a[j, r : r + SUB, :] = jnp.where(high_end, wrap[k], hi[0, k])
        for i in range(height // SUB):
            r = FIRST + i * SUB
            rows = slice(i * SUB, (i + 1) * SUB)
            lanes = slice(j * LANES, (j + 1) * LANES)
            mob[j, r : r + SUB, :] = 0.1 * mobility[rows, lanes]
            til[j, r : r + SUB, :] = tilt[rows, lanes]
    place(a, FIRST, msg, 0, height // SUB)
    run_cycle(a, b, mob, til, drift, 0, height)
    p[...] = a[:, FIRST - DEPTH : FIRST + height + DEPTH, :]


def off_kernel(msg, lo, hi, mob, til, drift, p, a, b):
    planes = a.shape[0]
    tiles = msg.shape[0] // planes
    height = tiles * SUB
    for ref in (a, b):
        blank(ref)
    place(a, FIRST - RIM, lo, 0, RIM // SUB)
    place(a, FIRST, msg, 0, tiles)
    place(a, FIRST + height, hi, 0, RIM // SUB)
    run_cycle(a, b, mob, til, drift, 0, height)
    p[...] = a[:, FIRST - DEPTH : FIRST + height + DEPTH, :]


def weights(msg):
    tile = msg[msg.shape[0] - 1]
    half = SUB // 2
    return jnp.broadcast_to(tile[0:1, :], tile.shape), jnp.broadcast_to(tile[half : half + 1, :], tile.shape)


def own_weights(msg):
    image = lax.axis_index("ladder")
    even = image % 2 == 0
    at_end = (image == 0) | (image == lax.axis_size("ladder") - 1)
    lower, upper = weights(msg)
    off = jnp.where(even, lower, upper)
    on = jnp.where(even, upper, lower)
    rest = 1.0 - lower - upper
    return jnp.where(at_end, rest + off, rest), jnp.where(at_end, 0.0, off), on


def off_weights(msg):
    even = lax.axis_index("ladder") % 2 == 0
    lower, upper = weights(msg)
    return 1.0 - lower - upper, jnp.where(even, upper, lower), jnp.where(even, lower, upper)


def second_kernel(which, msg, mid, one, two, mob, til, drift, q, a, b):
    planes, height, _ = q.shape
    for ref in (a, b):
        blank(ref)
    w = which(msg)
    for j in range(planes):
        for r in range(0, mid.shape[1], SUB):
            at = FIRST - DEPTH + r
            rows = slice(r, r + SUB)
            a[j, at : at + SUB, :] = w[0] * mid[j, rows, :] + w[1] * one[j, rows, :] + w[2] * two[j, rows, :]
    run_cycle(a, b, mob, til, drift, 1, height)
    q[...] = a[:, FIRST : FIRST + height, :]


def blend_kernel(msg, mid, one, two, out):
    w = own_weights(msg)
    for j in range(mid.shape[0]):
        for r in range(0, mid.shape[1], SUB):
            rows = slice(r, r + SUB)
            out[rows, j * LANES : (j + 1) * LANES] = (
                w[0] * mid[j, rows, :] + w[1] * one[j, rows, :] + w[2] * two[j, rows, :]
            )


VMEM = pl.BlockSpec(memory_space=pltpu.VMEM)


def call(kernel, name, operands, shapes, scratch=(), ops=10**3):
    out = [jax.ShapeDtypeStruct(s, jnp.float32) for s in shapes]
    single = len(out) == 1
    return pl.pallas_call(
        kernel,
        out_shape=out[0] if single else out,
        in_specs=[VMEM] * len(operands),
        out_specs=VMEM if single else [VMEM] * len(out),
        scratch_shapes=[pltpu.VMEM(s, jnp.float32) for s in scratch],
        compiler_params=pltpu.CompilerParams(vmem_limit_bytes=6 * 2**20),
        cost_estimate=pl.CostEstimate(flops=ops, bytes_accessed=2**10, transcendentals=0),
        name=name,
    )(*operands)


def body(initial, mobility, tilt, drift, mix_weights):
    ladder = lax.axis_size("ladder")
    space = lax.axis_size("space")
    height, cols = initial.shape[1:]
    planes = cols // LANES
    work = (planes, height + 2 * RIM + 24, LANES)
    wide = (planes, height + 2 * DEPTH, LANES)
    slab = (planes, height, LANES)
    rim = (planes * RIM // SUB, SUB, LANES)

    def off(i):
        return (i - 1) % ladder if i % 2 == 0 else (i + 1) % ladder

    def beyond(i):
        return (i - 3) % ladder if i % 2 == 0 else (i + 3) % ladder

    swap_off = [(i, off(i)) for i in range(ladder)]
    swap_on = [(i, i ^ 1) for i in range(ladder)]
    swap_beyond = [(i, beyond(i)) for i in range(ladder)]
    swap_ends = [(0, space - 1), (space - 1, 0)]
    both = ("ladder", "space")
    rise = [
        (i * space + s, i * space + s + 1 if s < space - 1 else off(i) * space)
        for i in range(ladder)
        for s in range(space)
    ]
    fall = [(b, a) for a, b in rise]

    half = SUB // 2
    tiles = initial.reshape(height // SUB, SUB, planes, LANES).transpose(0, 2, 1, 3).reshape(-1, SUB, LANES)
    pair = jnp.broadcast_to(mix_weights.reshape(2, 1, 1), (2, half, LANES)).reshape(1, SUB, LANES)
    msg = jnp.concatenate([tiles, pair])
    other = lax.ppermute(msg, "ladder", swap_off)
    flow = drift.reshape(planes, LANES)

    up, down, wrap = call(edges_kernel, "edges", (msg, mobility, tilt), [(3, *rim), (3, *rim), rim])
    wrap = lax.ppermute(wrap, "space", swap_ends)
    lo = lax.ppermute(up, both, rise)
    hi = lax.ppermute(down, both, fall)
    p_own, mob, til = call(
        own_kernel,
        "own_first",
        (msg, lo, hi, wrap, mobility, tilt, flow),
        [wide, work, work],
        [work, work],
    )
    p_own, other = lax.optimization_barrier((p_own, other))
    up, down = call(off_edges_kernel, "off_edges", (msg, other), [rim] * 2)
    p_own, up, down = lax.optimization_barrier((p_own, up, down))
    lo = lax.ppermute(up, both, rise)
    hi = lax.ppermute(down, both, fall)
    p_on = lax.ppermute(p_own, "ladder", swap_on)
    p_off = call(off_kernel, "off_first", (other, lo, hi, mob, til, flow), [wide], [work, work])
    p_beyond = lax.ppermute(p_off, "ladder", swap_beyond)

    q_own = call(
        functools.partial(second_kernel, own_weights),
        "own_second",
        (msg, p_own, p_off, p_on, mob, til, flow),
        [slab],
        [work, work],
        10**8,
    )
    q_on = lax.ppermute(q_own, "ladder", swap_on)
    q_off = call(
        functools.partial(second_kernel, off_weights),
        "off_second",
        (other, p_off, p_own, p_beyond, mob, til, flow),
        [slab],
        [work, work],
        10**8,
    )
    path = call(blend_kernel, "blend", (msg, q_own, q_off, q_on), [(height, cols)])
    return path[None]


def solution(mesh):
    in_specs = (
        P("ladder", "space", None),
        P("space", None),
        P("space", None),
        P(),
        P("ladder", None),
    )
    out_specs = P("ladder", "space", None)
    return jax.shard_map(body, mesh=mesh, in_specs=in_specs, out_specs=out_specs, check_vma=False)
```

time: 128 us -> 101 us (0.79)
  starting transfers between devices: 63.9 us -> 52.8 us
  local copies, waits for them, and re-layouts: 10.2 us -> 0.95 us
  between operations: 7.79 us -> 0.16 us
  waiting for transfers between devices: 23.8 us -> 25.9 us
    ppermute x8 -> x6, starting transfers between devices: 51.8 us -> 41.8 us  [the longest x2 22.2 us: body(): hi = lax.ppermute(down, both, fall)]
    unnamed x30 -> x8, local copies, waits for them, and re-layouts: 8.34 us -> 0.73 us
    ppermute x1, starting transfers between devices: 5.96 us -> 2.55 us  [body(): p_on = lax.ppermute(p_own, 'ladder', swap_on)]
    ppermute x8 -> x6, waiting for transfers between devices: 23.8 us -> 25.9 us  [the longest x1 22.1 us: body(): wrap = lax.ppermute(wrap, 'space', swap_ends)]
    slice x3 -> x0, local copies, waits for them, and re-layouts: 1.84 us -> none  [the longest x1 0.7 us: body(): own[:RIM]]
    ppermute x1, starting transfers between devices: 1.92 us -> 3.48 us  [body(): q_on = lax.ppermute(q_own, 'ladder', swap_on)]
    another operation x3 -> x0, other arithmetic: 1.46 us -> none  [the longest x1 1.3 us: body(): coeffs = jnp.stack([mobility, tilt])]
    pallas_call x5 -> x7, Pallas kernels: 19.1 us -> 19.8 us  [call(): pl.pallas_call(kernel, out_shape=out[0] if single else out, in_specs=[VME...]
  transfers between devices with their start and end apart: 11 -> 9, of which waited for: 3 -> 2; matrix products, arithmetic and copies ran while one was open for 2% -> 0% of each run, Pallas kernels for 14% -> 19%
where the time goes in v2:
time: 101 us
  starting transfers between devices  52.8 us (52%)
  waiting for transfers between devices  25.9 us (26%)
  Pallas kernels  19.8 us (20%)
  other arithmetic  1.03 us (1%)
    ppermute x2, starting transfers between devices, body(): hi = lax.ppermute(down, both, fall)  22.2 us
    ppermute x1, waiting for transfers between devices, body(): wrap = lax.ppermute(wrap, 'space', swap_ends)  22.1 us
    pallas_call x7, Pallas kernels, call(): pl.pallas_call(kernel, out_shape=out[0] if single else out, in_specs=[VME...  19.8 us
    ppermute x1, starting transfers between devices, body(): other = lax.ppermute(msg, 'ladder', swap_off)  8.83 us
    ppermute x2, starting transfers between devices, body(): lo = lax.ppermute(up, both, rise)  5.95 us
    ppermute x1, starting transfers between devices, body(): p_beyond = lax.ppermute(p_off, 'ladder', swap_beyond)  5.01 us
    ppermute x1, starting transfers between devices, body(): wrap = lax.ppermute(wrap, 'space', swap_ends)  4.79 us
    ppermute x2, waiting for transfers between devices, body(): lo = lax.ppermute(up, both, rise)  3.73 us
  transfers between devices with their start and end apart: 9, of which 2 were waited for; matrix products, arithmetic and copies ran while one was open for 0% of the time, Pallas kernels for 19%

profile of v2, /device:TPU:1, one launch (start us, length us, event | category | flops | bytes accessed | tf_op | source)
XLA Modules:
  0.0 100.7 jit_solution(6136198435841413463)
XLA Ops:
  0.0 0.7 copy-done.3
  0.7 0.1 broadcast_in_dim.15
  0.7 0.1 broadcast_in_dim.16
  0.8 0.1 broadcast_in_dim.17
  0.9 1.0 %pad_maximum_fusion.msg = f32[65,8,128]{2,1,0:T(8,128)S(1)} fusion(f32[1,8,128]{2,1,0:T(8,128)S(1)} %broadcast_in_dim.17, f32[64,8,128]{2,1,0:T(8,128)} %bitcast.12), kind=kLoop, calls=%fused_computation | loop fusion | flops 66560 | bytes 532480 | tf_op jit(solution)/shard_map/concatenate | solution.py:263
  1.9 0.1 copy-done.1
  2.0 0.1 edges.1
  2.1 4.0 %collective-permute-start = (f32[3,48,8,128]{3,2,1,0:T(8,128)S(1)}, f32[3,48,8,128]{3,2,1,0:T(8,128)S(1)}, u32[]{:S(2)}, u32[]{:S(2)}) collective-permute-start(f32[3,48,8,128]{3,2,1,0:T(8,128)S(1)} %get-tuple-element.18), channel_id=1, source_target_pairs={{0,1},{1,2},{2,3},{3,4},{4,5},{5,6},{6,7},{7,8},{8,9},{9,10},{10,1... | collective-permute-start | bytes 1769480 | tf_op jit(solution)/shard_map/ppermute | solution.py:269
  6.1 12.8 %collective-permute-start.1 = (f32[3,48,8,128]{3,2,1,0:T(8,128)S(1)}, f32[3,48,8,128]{3,2,1,0:T(8,128)S(1)}, u32[]{:S(2)}, u32[]{:S(2)}) collective-permute-start(f32[3,48,8,128]{3,2,1,0:T(8,128)S(1)} %get-tuple-element.19), channel_id=1, source_target_pairs={{1,0},{2,1},{3,2},{4,3},{5,4},{6,5},{7,6},{8,7},{9,8},{10,9},{11,1... | collective-permute-start | bytes 1769480 | tf_op jit(solution)/shard_map/ppermute | solution.py:270
  19.0 8.8 %collective-permute-start.3 = (f32[65,8,128]{2,1,0:T(8,128)S(1)}, f32[65,8,128]{2,1,0:T(8,128)S(1)}, u32[]{:S(2)}, u32[]{:S(2)}) collective-permute-start(f32[65,8,128]{2,1,0:T(8,128)S(1)} %pad_maximum_fusion.msg), channel_id=1, source_target_pairs={{0,480},{32,64},{64,32},{96,128},{128,96},{160,192},{192,160},{224... | collective-permute-start | bytes 798728 | tf_op jit(solution)/shard_map/ppermute | solution.py:264
  27.8 4.8 %collective-permute-start.2 = (f32[48,8,128]{2,1,0:T(8,128)S(1)}, f32[48,8,128]{2,1,0:T(8,128)S(1)}, u32[]{:S(2)}, u32[]{:S(2)}) collective-permute-start(f32[48,8,128]{2,1,0:T(8,128)S(1)} %get-tuple-element.20), channel_id=1, source_target_pairs={{0,31},{31,0},{32,63},{63,32},{64,95},{95,64},{96,127},{127,96},{1... | collective-permute-start | bytes 589832 | tf_op jit(solution)/shard_map/ppermute | solution.py:268
  32.6 22.1 %collective-permute-done.2.wrap = f32[48,8,128]{2,1,0:T(8,128)S(1)} collective-permute-done((f32[48,8,128]{2,1,0:T(8,128)S(1)}, f32[48,8,128]{2,1,0:T(8,128)S(1)}, u32[]{:S(2)}, u32[]{:S(2)}) %collective-permute-start.2) | collective-permute-done | bytes 196640 | tf_op jit(solution)/shard_map/ppermute | solution.py:268
  54.8 5.6 %own_first.1 = (f32[16,56,128]{2,1,0:T(8,128)S(1)}, f32[16,104,128]{2,1,0:T(8,128)S(1)}, f32[16,104,128]{2,1,0:T(8,128)S(1)}) custom-call(f32[65,8,128]{2,1,0:T(8,128)S(1)} %pad_maximum_fusion.msg, f32[3,48,8,128]{3,2,1,0:T(8,128)S(1)} %collective-permute-done.lo, f32[3,48,8,128]{3,2,1,0:T(8,128)S(1)} %collective-permute-done.1.hi, ...), custom_call_target="tpu_custom_call" | custom-call | flops 1000 | bytes 1024 | tf_op jit(solution)/shard_map/own_first/pallas_call | solution.py:220
  60.5 2.5 %collective-permute-start.6 = (f32[16,56,128]{2,1,0:T(8,128)S(1)}, f32[16,56,128]{2,1,0:T(8,128)S(1)}, u32[]{:S(2)}, u32[]{:S(2)}) collective-permute-start(f32[16,56,128]{2,1,0:T(8,128)S(1)} %get-tuple-element.26.mid.one), channel_id=1, source_target_pairs={{0,32},{32,0},{64,96},{96,64},{128,160},{160,128},{192,224},{224,1... | collective-permute-start | bytes 1376264 | tf_op jit(solution)/shard_map/ppermute | solution.py:283
  63.0 1.9 %collective-permute-start.4 = (f32[48,8,128]{2,1,0:T(8,128)S(1)}, f32[48,8,128]{2,1,0:T(8,128)S(1)}, u32[]{:S(2)}, u32[]{:S(2)}) collective-permute-start(f32[48,8,128]{2,1,0:T(8,128)S(1)} %get-tuple-element.27), channel_id=1, source_target_pairs={{0,1},{1,2},{2,3},{3,4},{4,5},{5,6},{6,7},{7,8},{8,9},{9,10},{10,1... | collective-permute-start | bytes 589832 | tf_op jit(solution)/shard_map/ppermute | solution.py:281
  64.9 9.4 %collective-permute-start.5 = (f32[48,8,128]{2,1,0:T(8,128)S(1)}, f32[48,8,128]{2,1,0:T(8,128)S(1)}, u32[]{:S(2)}, u32[]{:S(2)}) collective-permute-start(f32[48,8,128]{2,1,0:T(8,128)S(1)} %get-tuple-element.28), channel_id=1, source_target_pairs={{1,0},{2,1},{3,2},{4,3},{5,4},{6,5},{7,6},{8,7},{9,8},{10,9},{11,1... | collective-permute-start | bytes 589832 | tf_op jit(solution)/shard_map/ppermute | solution.py:282
  74.3 3.7 %collective-permute-done.4.lo = f32[48,8,128]{2,1,0:T(8,128)S(1)} collective-permute-done((f32[48,8,128]{2,1,0:T(8,128)S(1)}, f32[48,8,128]{2,1,0:T(8,128)S(1)}, u32[]{:S(2)}, u32[]{:S(2)}) %collective-permute-start.4) | collective-permute-done | bytes 196640 | tf_op jit(solution)/shard_map/ppermute | solution.py:281
  78.1 0.0 collective-permute-done.5.hi
  78.1 5.4 %off_first.1.one.mid = f32[16,56,128]{2,1,0:T(8,128)S(1)} custom-call(f32[65,8,128]{2,1,0:T(8,128)S(1)} %collective-permute-done.3.other.msg, f32[48,8,128]{2,1,0:T(8,128)S(1)} %collective-permute-done.4.lo, f32[48,8,128]{2,1,0:T(8,128)S(1)} %collective-permute-done.5.hi, f32[16,104,128]{2,1,0:T(8,128)S(1)} %get-tuple-element.29.mob, ...), custom_call_target="tpu_custom_call" | custom-call | flops 1000 | bytes 1024 | tf_op jit(solution)/shard_map/off_first/pallas_call | solution.py:220
  83.5 5.0 %collective-permute-start.7 = (f32[16,56,128]{2,1,0:T(8,128)S(1)}, f32[16,56,128]{2,1,0:T(8,128)S(1)}, u32[]{:S(2)}, u32[]{:S(2)}) collective-permute-start(f32[16,56,128]{2,1,0:T(8,128)S(1)} %off_first.1.one.mid), channel_id=1, source_target_pairs={{0,416},{32,128},{64,480},{96,192},{128,32},{160,256},{192,96},{22... | collective-permute-start | bytes 1376264 | tf_op jit(solution)/shard_map/ppermute | solution.py:285
  88.5 3.9 %own_second.1.mid = f32[16,32,128]{2,1,0:T(8,128)S(1)} custom-call(f32[65,8,128]{2,1,0:T(8,128)S(1)} %pad_maximum_fusion.msg, f32[16,56,128]{2,1,0:T(8,128)S(1)} %get-tuple-element.26.mid.one, f32[16,56,128]{2,1,0:T(8,128)S(1)} %off_first.1.one.mid, f32[16,56,128]{2,1,0:T(8,128)S(1)} %collective-permute-done.6.two, ...), custom_call_target="tpu_custom_call" | custom-call | flops 100000000 | bytes 1024 | tf_op jit(solution)/shard_map/own_second/pallas_call | solution.py:220
  92.5 3.5 %collective-permute-start.8 = (f32[16,32,128]{2,1,0:T(8,128)S(1)}, f32[16,32,128]{2,1,0:T(8,128)S(1)}, u32[]{:S(2)}, u32[]{:S(2)}) collective-permute-start(f32[16,32,128]{2,1,0:T(8,128)S(1)} %own_second.1.mid), channel_id=1, source_target_pairs={{0,32},{32,0},{64,96},{96,64},{128,160},{160,128},{192,224},{224,1... | collective-permute-start | bytes 786440 | tf_op jit(solution)/shard_map/ppermute | solution.py:295
  96.0 3.9 %off_second.1.one = f32[16,32,128]{2,1,0:T(8,128)S(1)} custom-call(f32[65,8,128]{2,1,0:T(8,128)S(1)} %collective-permute-done.3.other.msg, f32[16,56,128]{2,1,0:T(8,128)S(1)} %off_first.1.one.mid, f32[16,56,128]{2,1,0:T(8,128)S(1)} %get-tuple-element.26.mid.one, f32[16,56,128]{2,1,0:T(8,128)S(1)} %collective-permute-done.7.two, ...), custom_call_target="tpu_custom_call" | custom-call | flops 100000000 | bytes 1024 | tf_op jit(solution)/shard_map/off_second/pallas_call | solution.py:220
  99.9 0.8 blend.1
  (13 shorter events, 0.1 us)
Async XLA Ops:
  0.0 0.7 copy-start.3
  0.9 1.0 %copy-start = (f32[32,2048]{1,0:T(8,128)S(1)}, f32[32,2048]{1,0:T(8,128)}, u32[]{:S(2)}) copy-start(f32[32,2048]{1,0:T(8,128)} %mobility.3) | copy-start | bytes 786436
  0.9 1.1 %copy-start.1 = (f32[32,2048]{1,0:T(8,128)S(1)}, f32[32,2048]{1,0:T(8,128)}, u32[]{:S(2)}) copy-start(f32[32,2048]{1,0:T(8,128)} %tilt.3) | copy-start | bytes 786436
  2.0 52.8 %copy-start.2 = (f32[2048]{0:T(1024)S(1)}, f32[2048]{0:T(1024)}, u32[]{:S(2)}) copy-start(f32[2048]{0:T(1024)} %param.8) | copy-start | bytes 24580
  2.1 52.7 %collective-permute-start = (f32[3,48,8,128]{3,2,1,0:T(8,128)S(1)}, f32[3,48,8,128]{3,2,1,0:T(8,128)S(1)}, u32[]{:S(2)}, u32[]{:S(2)}) collective-permute-start(f32[3,48,8,128]{3,2,1,0:T(8,128)S(1)} %get-tuple-element.18), channel_id=1, source_target_pairs={{0,1},{1,2},{2,3},{3,4},{4,5},{5,6},{6,7},{7,8},{8,9},{9,10},{10,1... | collective-permute-start | bytes 1769480 | tf_op jit(solution)/shard_map/ppermute | solution.py:269
  6.1 48.6 %collective-permute-start.1 = (f32[3,48,8,128]{3,2,1,0:T(8,128)S(1)}, f32[3,48,8,128]{3,2,1,0:T(8,128)S(1)}, u32[]{:S(2)}, u32[]{:S(2)}) collective-permute-start(f32[3,48,8,128]{3,2,1,0:T(8,128)S(1)} %get-tuple-element.19), channel_id=1, source_target_pairs={{1,0},{2,1},{3,2},{4,3},{5,4},{6,5},{7,6},{8,7},{9,8},{10,9},{11,1... | collective-permute-start | bytes 1769480 | tf_op jit(solution)/shard_map/ppermute | solution.py:270
  19.0 41.4 %collective-permute-start.3 = (f32[65,8,128]{2,1,0:T(8,128)S(1)}, f32[65,8,128]{2,1,0:T(8,128)S(1)}, u32[]{:S(2)}, u32[]{:S(2)}) collective-permute-start(f32[65,8,128]{2,1,0:T(8,128)S(1)} %pad_maximum_fusion.msg), channel_id=1, source_target_pairs={{0,480},{32,64},{64,32},{96,128},{128,96},{160,192},{192,160},{224... | collective-permute-start | bytes 798728 | tf_op jit(solution)/shard_map/ppermute | solution.py:264
  27.8 26.9 %collective-permute-start.2 = (f32[48,8,128]{2,1,0:T(8,128)S(1)}, f32[48,8,128]{2,1,0:T(8,128)S(1)}, u32[]{:S(2)}, u32[]{:S(2)}) collective-permute-start(f32[48,8,128]{2,1,0:T(8,128)S(1)} %get-tuple-element.20), channel_id=1, source_target_pairs={{0,31},{31,0},{32,63},{63,32},{64,95},{95,64},{96,127},{127,96},{1... | collective-permute-start | bytes 589832 | tf_op jit(solution)/shard_map/ppermute | solution.py:268
  60.5 28.1 %collective-permute-start.6 = (f32[16,56,128]{2,1,0:T(8,128)S(1)}, f32[16,56,128]{2,1,0:T(8,128)S(1)}, u32[]{:S(2)}, u32[]{:S(2)}) collective-permute-start(f32[16,56,128]{2,1,0:T(8,128)S(1)} %get-tuple-element.26.mid.one), channel_id=1, source_target_pairs={{0,32},{32,0},{64,96},{96,64},{128,160},{160,128},{192,224},{224,1... | collective-permute-start | bytes 1376264 | tf_op jit(solution)/shard_map/ppermute | solution.py:283
  63.0 15.1 %collective-permute-start.4 = (f32[48,8,128]{2,1,0:T(8,128)S(1)}, f32[48,8,128]{2,1,0:T(8,128)S(1)}, u32[]{:S(2)}, u32[]{:S(2)}) collective-permute-start(f32[48,8,128]{2,1,0:T(8,128)S(1)} %get-tuple-element.27), channel_id=1, source_target_pairs={{0,1},{1,2},{2,3},{3,4},{4,5},{5,6},{6,7},{7,8},{8,9},{9,10},{10,1... | collective-permute-start | bytes 589832 | tf_op jit(solution)/shard_map/ppermute | solution.py:281
  64.9 13.1 %collective-permute-start.5 = (f32[48,8,128]{2,1,0:T(8,128)S(1)}, f32[48,8,128]{2,1,0:T(8,128)S(1)}, u32[]{:S(2)}, u32[]{:S(2)}) collective-permute-start(f32[48,8,128]{2,1,0:T(8,128)S(1)} %get-tuple-element.28), channel_id=1, source_target_pairs={{1,0},{2,1},{3,2},{4,3},{5,4},{6,5},{7,6},{8,7},{9,8},{10,9},{11,1... | collective-permute-start | bytes 589832 | tf_op jit(solution)/shard_map/ppermute | solution.py:282
  83.5 12.4 %collective-permute-start.7 = (f32[16,56,128]{2,1,0:T(8,128)S(1)}, f32[16,56,128]{2,1,0:T(8,128)S(1)}, u32[]{:S(2)}, u32[]{:S(2)}) collective-permute-start(f32[16,56,128]{2,1,0:T(8,128)S(1)} %off_first.1.one.mid), channel_id=1, source_target_pairs={{0,416},{32,128},{64,480},{96,192},{128,32},{160,256},{192,96},{22... | collective-permute-start | bytes 1376264 | tf_op jit(solution)/shard_map/ppermute | solution.py:285
  92.5 7.4 %collective-permute-start.8 = (f32[16,32,128]{2,1,0:T(8,128)S(1)}, f32[16,32,128]{2,1,0:T(8,128)S(1)}, u32[]{:S(2)}, u32[]{:S(2)}) collective-permute-start(f32[16,32,128]{2,1,0:T(8,128)S(1)} %own_second.1.mid), channel_id=1, source_target_pairs={{0,32},{32,0},{64,96},{96,64},{128,160},{160,128},{192,224},{224,1... | collective-permute-start | bytes 786440 | tf_op jit(solution)/shard_map/ppermute | solution.py:295

commit v3 on v2

--- a/solution.py
+++ b/solution.py
@@ -14,11 +14,8 @@
 FIRST = 36
 
 
-def spans(k, cycle, height):
-    rim = RIM - DEPTH * cycle
-    begin = FIRST - rim + k
-    end = FIRST + height + rim - k
-    return begin // SUB, -(-end // SUB)
+def spans(k, begin, end):
+    return (begin + k) // SUB, -(-(end - k) // SUB)
 
 
 def sweep(src, dst, mob, tilt, drift, span):
@@ -46,12 +43,12 @@
             dst[j, r : r + SUB, :] = (f + gain) + speed * (jnp.where(rising, below, above) - f)
 
 
-def run_cycle(a, b, mob, tilt, drift, cycle, height):
+def run_cycle(a, b, mob, tilt, drift, begin, end):
     k = 1
     while k <= DEPTH:
-        span = spans(k, cycle, height)
+        span = spans(k, begin, end)
         last = k
-        while last < DEPTH and spans(last + 1, cycle, height) == span:
+        while last < DEPTH and spans(last + 1, begin, end) == span:
             last += 1
         if k % 2 == 0:
             sweep(b, a, mob, tilt, drift, span)
@@ -86,8 +83,7 @@
         ref[j, rows - 16 : rows, :] = jnp.zeros((16, LANES), jnp.float32)
 
 
-def edges_kernel(msg, mobility, tilt, up, down, wrap):
-    low_end = lax.axis_index("space") == 0
+def edges_kernel(msg, mobility, tilt, down, up):
     planes = mobility.shape[1] // LANES
     tiles = mobility.shape[0] // SUB
     count = RIM // SUB
@@ -95,32 +91,32 @@
     for i in range(count):
         for j in range(planes):
             k = i * planes + j
-            top = msg[k + skip * planes]
-            bottom = msg[k]
-            wrap[k] = jnp.where(low_end, bottom, top)
             lanes = slice(j * LANES, (j + 1) * LANES)
             lo = slice(i * SUB, (i + 1) * SUB)
             hi = slice((i + skip) * SUB, (i + skip + 1) * SUB)
-            up[0, k] = top
+            up[0, k] = msg[k + skip * planes]
             up[1, k] = mobility[hi, lanes]
             up[2, k] = tilt[hi, lanes]
-            down[0, k] = bottom
+            down[0, k] = msg[k]
             down[1, k] = mobility[lo, lanes]
             down[2, k] = tilt[lo, lanes]
 
 
-def off_edges_kernel(msg, other, up, down):
+def off_edges_kernel(msg, other, down, up, ends):
     slab = lax.axis_index("space")
     low_end = slab == 0
     high_end = slab == lax.axis_size("space") - 1
     count = up.shape[0]
     skip = other.shape[0] - 1 - count
     for k in range(count):
-        up[k] = jnp.where(high_end, msg[k + skip], other[k + skip])
-        down[k] = jnp.where(low_end, msg[k], other[k])
-
-
-def own_kernel(msg, lo, hi, wrap, mobility, tilt, drift, p, mob, til, a, b):
+        top = other[k + skip]
+        bottom = other[k]
+        up[k] = jnp.where(high_end, msg[k + skip], top)
+        down[k] = jnp.where(low_end, msg[k], bottom)
+        ends[k] = jnp.where(low_end, bottom, top)
+
+
+def own_kernel(msg, hi, lo, ends, mobility, tilt, drift, p, mob, til, a, b):
     slab = lax.axis_index("space")
     low_end = slab == 0
     high_end = slab == lax.axis_size("space") - 1
@@ -132,26 +128,23 @@
     for j in range(planes):
         for i in range(count):
             k = i * planes + j
-            for at, got in ((FIRST - RIM, lo), (FIRST + height, hi)):
-                r = at + i * SUB
-                mob[j, r : r + SUB, :] = 0.1 * got[1, k]
-                til[j, r : r + SUB, :] = got[2, k]
-            r = FIRST - RIM + i * SUB
-            a[j, r : r + SUB, :] = jnp.where(low_end, wrap[k], lo[0, k])
-            r = FIRST + height + i * SUB
-            a[j, r : r + SUB, :] = jnp.where(high_end, wrap[k], hi[0, k])
+            for at, got, alone in ((FIRST - RIM, lo, low_end), (FIRST + height, hi, high_end)):
+                rows = slice(at + i * SUB, at + (i + 1) * SUB)
+                a[j, rows, :] = jnp.where(alone, ends[k], got[0, k])
+                mob[j, rows, :] = 0.1 * got[1, k]
+                til[j, rows, :] = got[2, k]
         for i in range(height // SUB):
-            r = FIRST + i * SUB
+            at = FIRST + i * SUB
             rows = slice(i * SUB, (i + 1) * SUB)
             lanes = slice(j * LANES, (j + 1) * LANES)
-            mob[j, r : r + SUB, :] = 0.1 * mobility[rows, lanes]
-            til[j, r : r + SUB, :] = tilt[rows, lanes]
+            mob[j, at : at + SUB, :] = 0.1 * mobility[rows, lanes]
+            til[j, at : at + SUB, :] = tilt[rows, lanes]
     place(a, FIRST, msg, 0, height // SUB)
-    run_cycle(a, b, mob, til, drift, 0, height)
+    run_cycle(a, b, mob, til, drift, FIRST - RIM, FIRST + height + RIM)
     p[...] = a[:, FIRST - DEPTH : FIRST + height + DEPTH, :]
 
 
-def off_kernel(msg, lo, hi, mob, til, drift, p, a, b):
+def off_kernel(msg, hi, lo, mob, til, drift, p, a, b):
     planes = a.shape[0]
     tiles = msg.shape[0] // planes
     height = tiles * SUB
@@ -160,7 +153,7 @@
     place(a, FIRST - RIM, lo, 0, RIM // SUB)
     place(a, FIRST, msg, 0, tiles)
     place(a, FIRST + height, hi, 0, RIM // SUB)
-    run_cycle(a, b, mob, til, drift, 0, height)
+    run_cycle(a, b, mob, til, drift, FIRST - RIM, FIRST + height + RIM)
     p[...] = a[:, FIRST - DEPTH : FIRST + height + DEPTH, :]
 
 
@@ -197,7 +190,7 @@
             at = FIRST - DEPTH + r
             rows = slice(r, r + SUB)
             a[j, at : at + SUB, :] = w[0] * mid[j, rows, :] + w[1] * one[j, rows, :] + w[2] * two[j, rows, :]
-    run_cycle(a, b, mob, til, drift, 1, height)
+    run_cycle(a, b, mob, til, drift, FIRST - DEPTH, FIRST + height + DEPTH)
     q[...] = a[:, FIRST : FIRST + height, :]
 
 
@@ -248,7 +241,6 @@
     swap_off = [(i, off(i)) for i in range(ladder)]
     swap_on = [(i, i ^ 1) for i in range(ladder)]
     swap_beyond = [(i, beyond(i)) for i in range(ladder)]
-    swap_ends = [(0, space - 1), (space - 1, 0)]
     both = ("ladder", "space")
     rise = [
         (i * space + s, i * space + s + 1 if s < space - 1 else off(i) * space)
@@ -256,6 +248,7 @@
         for s in range(space)
     ]
     fall = [(b, a) for a, b in rise]
+    at_ends = [(i * space + s, off(i) * space + space - 1 - s) for i in range(ladder) for s in (0, space - 1)]
 
     half = SUB // 2
     tiles = initial.reshape(height // SUB, SUB, planes, LANES).transpose(0, 2, 1, 3).reshape(-1, SUB, LANES)
@@ -264,24 +257,23 @@
     other = lax.ppermute(msg, "ladder", swap_off)
     flow = drift.reshape(planes, LANES)
 
-    up, down, wrap = call(edges_kernel, "edges", (msg, mobility, tilt), [(3, *rim), (3, *rim), rim])
-    wrap = lax.ppermute(wrap, "space", swap_ends)
+    down, up = call(edges_kernel, "edges", (msg, mobility, tilt), [(3, *rim)] * 2)
+    own_hi = lax.ppermute(down, both, fall)
+    own_lo = lax.ppermute(up, both, rise)
+    down, up, ends = call(off_edges_kernel, "off_edges", (msg, other), [rim] * 3, ops=4 * 10**10)
+    hi = lax.ppermute(down, both, fall)
     lo = lax.ppermute(up, both, rise)
-    hi = lax.ppermute(down, both, fall)
+    ends = lax.ppermute(ends, both, at_ends)
     p_own, mob, til = call(
         own_kernel,
         "own_first",
-        (msg, lo, hi, wrap, mobility, tilt, flow),
+        (msg, own_hi, own_lo, ends, mobility, tilt, flow),
         [wide, work, work],
         [work, work],
+        5 * 10**9,
     )
-    p_own, other = lax.optimization_barrier((p_own, other))
-    up, down = call(off_edges_kernel, "off_edges", (msg, other), [rim] * 2)
-    p_own, up, down = lax.optimization_barrier((p_own, up, down))
-    lo = lax.ppermute(up, both, rise)
-    hi = lax.ppermute(down, both, fall)
     p_on = lax.ppermute(p_own, "ladder", swap_on)
-    p_off = call(off_kernel, "off_first", (other, lo, hi, mob, til, flow), [wide], [work, work])
+    p_off = call(off_kernel, "off_first", (other, hi, lo, mob, til, flow), [wide], [work, work], 5 * 10**9)
     p_beyond = lax.ppermute(p_off, "ladder", swap_beyond)
 
     q_own = call(
@@ -290,7 +282,7 @@
         (msg, p_own, p_off, p_on, mob, til, flow),
         [slab],
         [work, work],
-        10**8,
+        4 * 10**9,
     )
     q_on = lax.ppermute(q_own, "ladder", swap_on)
     q_off = call(
@@ -299,7 +291,7 @@
         (other, p_off, p_own, p_beyond, mob, til, flow),
         [slab],
         [work, work],
-        10**8,
+        4 * 10**9,
     )
     path = call(blend_kernel, "blend", (msg, q_own, q_off, q_on), [(height, cols)])
     return path[None]

time: 101 us -> 91.2 us (0.903)
  waiting for transfers between devices: 25.9 us -> 9.35 us
  starting transfers between devices: 52.8 us -> 59.9 us
    ppermute x1 -> x3, starting transfers between devices: 4.79 us -> 28.3 us  [the longest x1 22.5 us: body(): ends = lax.ppermute(ends, both, at_ends)]
    ppermute x2 -> x1, starting transfers between devices: 22.2 us -> 1.92 us  [body(): hi = lax.ppermute(down, both, fall)]
    ppermute x1 -> x3, waiting for transfers between devices: 22.1 us -> 7.55 us  [the longest x1 7.54 us: body(): ends = lax.ppermute(ends, both, at_ends)]
    ppermute x1, starting transfers between devices: 8.83 us -> 16.8 us  [body(): other = lax.ppermute(msg, 'ladder', swap_off)]
    ppermute x2 -> x1, waiting for transfers between devices: 3.73 us -> 0.01 us  [body(): lo = lax.ppermute(up, both, rise)]
    ppermute x1, starting transfers between devices: 5.01 us -> 1.92 us  [body(): p_beyond = lax.ppermute(p_off, 'ladder', swap_beyond)]
    ppermute x2 -> x1, starting transfers between devices: 5.95 us -> 3.36 us  [body(): lo = lax.ppermute(up, both, rise)]
    ppermute x1, starting transfers between devices: 2.55 us -> 4.59 us  [body(): p_on = lax.ppermute(p_own, 'ladder', swap_on)]
  transfers between devices with their start and end apart: 9 -> 9, of which waited for: 2 -> 3; matrix products, arithmetic and copies ran while one was open for 0% -> 0% of each run, Pallas kernels for 19% -> 21%
where the time goes in v3:
time: 91.2 us; the launch traced here: 90.8 us
  starting transfers between devices  59.9 us (66%)
  Pallas kernels  19.5 us (21%)
  waiting for transfers between devices  9.35 us (10%)
  other arithmetic  1.03 us (1%)
    ppermute x1, starting transfers between devices, body(): ends = lax.ppermute(ends, both, at_ends)  22.5 us
    pallas_call x7, Pallas kernels, call(): pl.pallas_call(kernel, out_shape=out[0] if single else out, in_specs=[VME...  19.5 us
    ppermute x1, starting transfers between devices, body(): other = lax.ppermute(msg, 'ladder', swap_off)  16.8 us
    ppermute x1, waiting for transfers between devices, body(): ends = lax.ppermute(ends, both, at_ends)  7.54 us
    ppermute x1, starting transfers between devices, body(): p_on = lax.ppermute(p_own, 'ladder', swap_on)  4.59 us
    ppermute x1, starting transfers between devices, body(): own_hi = lax.ppermute(down, both, fall)  3.91 us
    ppermute x1, starting transfers between devices, body(): lo = lax.ppermute(up, both, rise)  3.36 us
    ppermute x1, starting transfers between devices, body(): q_on = lax.ppermute(q_own, 'ladder', swap_on)  2.94 us
  transfers between devices with their start and end apart: 9, of which 3 were waited for; matrix products, arithmetic and copies ran while one was open for 0% of the time, Pallas kernels for 21%

profile of v3, /device:TPU:1, one launch (start us, length us, event | category | flops | bytes accessed | tf_op | source)
XLA Modules:
  0.0 90.8 jit_solution(13485513466098522062)
XLA Ops:
  0.0 0.7 copy-done.3
  0.7 0.1 broadcast_in_dim.15
  0.7 0.1 broadcast_in_dim.16
  0.8 0.1 broadcast_in_dim.17
  0.9 1.0 %pad_maximum_fusion.msg = f32[65,8,128]{2,1,0:T(8,128)S(1)} fusion(f32[1,8,128]{2,1,0:T(8,128)S(1)} %broadcast_in_dim.17, f32[64,8,128]{2,1,0:T(8,128)} %bitcast.12), kind=kLoop, calls=%fused_computation | loop fusion | flops 66560 | bytes 532480 | tf_op jit(solution)/shard_map/concatenate | solution.py:256
  1.9 16.8 %collective-permute-start.2 = (f32[65,8,128]{2,1,0:T(8,128)S(1)}, f32[65,8,128]{2,1,0:T(8,128)S(1)}, u32[]{:S(2)}, u32[]{:S(2)}) collective-permute-start(f32[65,8,128]{2,1,0:T(8,128)S(1)} %pad_maximum_fusion.msg), channel_id=1, source_target_pairs={{0,480},{32,64},{64,32},{96,128},{128,96},{160,192},{192,160},{224... | collective-permute-start | bytes 798728 | tf_op jit(solution)/shard_map/ppermute | solution.py:257
  18.8 0.1 edges.1
  18.9 3.9 %collective-permute-start = (f32[3,48,8,128]{3,2,1,0:T(8,128)S(1)}, f32[3,48,8,128]{3,2,1,0:T(8,128)S(1)}, u32[]{:S(2)}, u32[]{:S(2)}) collective-permute-start(f32[3,48,8,128]{3,2,1,0:T(8,128)S(1)} %get-tuple-element.13), channel_id=1, source_target_pairs={{1,0},{2,1},{3,2},{4,3},{5,4},{6,5},{7,6},{8,7},{9,8},{10,9},{11,1... | collective-permute-start | bytes 1769480 | tf_op jit(solution)/shard_map/ppermute | solution.py:261
  22.8 1.9 %collective-permute-start.1 = (f32[3,48,8,128]{3,2,1,0:T(8,128)S(1)}, f32[3,48,8,128]{3,2,1,0:T(8,128)S(1)}, u32[]{:S(2)}, u32[]{:S(2)}) collective-permute-start(f32[3,48,8,128]{3,2,1,0:T(8,128)S(1)} %get-tuple-element.14), channel_id=1, source_target_pairs={{0,1},{1,2},{2,3},{3,4},{4,5},{5,6},{6,7},{7,8},{8,9},{9,10},{10,1... | collective-permute-start | bytes 1769480 | tf_op jit(solution)/shard_map/ppermute | solution.py:262
  24.7 0.4 collective-permute-done.2.other.msg
  25.1 0.1 off_edges.1
  25.2 22.5 %collective-permute-start.3 = (f32[48,8,128]{2,1,0:T(8,128)S(1)}, f32[48,8,128]{2,1,0:T(8,128)S(1)}, u32[]{:S(2)}, u32[]{:S(2)}) collective-permute-start(f32[48,8,128]{2,1,0:T(8,128)S(1)} %get-tuple-element.15), channel_id=1, source_target_pairs={{0,511},{31,480},{32,95},{63,64},{64,63},{95,32},{96,159},{127,128... | collective-permute-start | bytes 589832 | tf_op jit(solution)/shard_map/ppermute | solution.py:266
  47.7 1.9 %collective-permute-start.4 = (f32[48,8,128]{2,1,0:T(8,128)S(1)}, f32[48,8,128]{2,1,0:T(8,128)S(1)}, u32[]{:S(2)}, u32[]{:S(2)}) collective-permute-start(f32[48,8,128]{2,1,0:T(8,128)S(1)} %get-tuple-element.17), channel_id=1, source_target_pairs={{1,0},{2,1},{3,2},{4,3},{5,4},{6,5},{7,6},{8,7},{9,8},{10,9},{11,1... | collective-permute-start | bytes 589832 | tf_op jit(solution)/shard_map/ppermute | solution.py:264
  49.6 3.4 %collective-permute-start.5 = (f32[48,8,128]{2,1,0:T(8,128)S(1)}, f32[48,8,128]{2,1,0:T(8,128)S(1)}, u32[]{:S(2)}, u32[]{:S(2)}) collective-permute-start(f32[48,8,128]{2,1,0:T(8,128)S(1)} %get-tuple-element.18), channel_id=1, source_target_pairs={{0,1},{1,2},{2,3},{3,4},{4,5},{5,6},{6,7},{7,8},{8,9},{9,10},{10,1... | collective-permute-start | bytes 589832 | tf_op jit(solution)/shard_map/ppermute | solution.py:265
  53.0 7.5 %collective-permute-done.3.ends = f32[48,8,128]{2,1,0:T(8,128)S(1)} collective-permute-done((f32[48,8,128]{2,1,0:T(8,128)S(1)}, f32[48,8,128]{2,1,0:T(8,128)S(1)}, u32[]{:S(2)}, u32[]{:S(2)}) %collective-permute-start.3) | collective-permute-done | bytes 196640 | tf_op jit(solution)/shard_map/ppermute | solution.py:266
  60.5 5.6 %own_first.1 = (f32[16,56,128]{2,1,0:T(8,128)S(1)}, f32[16,104,128]{2,1,0:T(8,128)S(1)}, f32[16,104,128]{2,1,0:T(8,128)S(1)}) custom-call(f32[65,8,128]{2,1,0:T(8,128)S(1)} %pad_maximum_fusion.msg, f32[3,48,8,128]{3,2,1,0:T(8,128)S(1)} %collective-permute-done.hi, f32[3,48,8,128]{3,2,1,0:T(8,128)S(1)} %collective-permute-done.1.lo, ...), custom_call_target="tpu_custom_call" | custom-call | flops 5000000000 | bytes 1024 | tf_op jit(solution)/shard_map/own_first/pallas_call | solution.py:213
  66.1 4.6 %collective-permute-start.6 = (f32[16,56,128]{2,1,0:T(8,128)S(1)}, f32[16,56,128]{2,1,0:T(8,128)S(1)}, u32[]{:S(2)}, u32[]{:S(2)}) collective-permute-start(f32[16,56,128]{2,1,0:T(8,128)S(1)} %get-tuple-element.16.mid.one), channel_id=1, source_target_pairs={{0,32},{32,0},{64,96},{96,64},{128,160},{160,128},{192,224},{224,1... | collective-permute-start | bytes 1376264 | tf_op jit(solution)/shard_map/ppermute | solution.py:275
  70.7 5.4 %off_first.1.one.mid = f32[16,56,128]{2,1,0:T(8,128)S(1)} custom-call(f32[65,8,128]{2,1,0:T(8,128)S(1)} %collective-permute-done.2.other.msg, f32[48,8,128]{2,1,0:T(8,128)S(1)} %collective-permute-done.4.hi, f32[48,8,128]{2,1,0:T(8,128)S(1)} %collective-permute-done.5.lo, f32[16,104,128]{2,1,0:T(8,128)S(1)} %get-tuple-element.19.mob, ...), custom_call_target="tpu_custom_call" | custom-call | flops 5000000000 | bytes 1024 | tf_op jit(solution)/shard_map/off_first/pallas_call | solution.py:213
  76.1 1.9 %collective-permute-start.7 = (f32[16,56,128]{2,1,0:T(8,128)S(1)}, f32[16,56,128]{2,1,0:T(8,128)S(1)}, u32[]{:S(2)}, u32[]{:S(2)}) collective-permute-start(f32[16,56,128]{2,1,0:T(8,128)S(1)} %off_first.1.one.mid), channel_id=1, source_target_pairs={{0,416},{32,128},{64,480},{96,192},{128,32},{160,256},{192,96},{22... | collective-permute-start | bytes 1376264 | tf_op jit(solution)/shard_map/ppermute | solution.py:277
  78.0 3.8 %own_second.1.mid = f32[16,32,128]{2,1,0:T(8,128)S(1)} custom-call(f32[65,8,128]{2,1,0:T(8,128)S(1)} %pad_maximum_fusion.msg, f32[16,56,128]{2,1,0:T(8,128)S(1)} %get-tuple-element.16.mid.one, f32[16,56,128]{2,1,0:T(8,128)S(1)} %off_first.1.one.mid, f32[16,56,128]{2,1,0:T(8,128)S(1)} %collective-permute-done.6.two, ...), custom_call_target="tpu_custom_call" | custom-call | flops 4000000000 | bytes 1024 | tf_op jit(solution)/shard_map/own_second/pallas_call | solution.py:213
  81.8 2.9 %collective-permute-start.8 = (f32[16,32,128]{2,1,0:T(8,128)S(1)}, f32[16,32,128]{2,1,0:T(8,128)S(1)}, u32[]{:S(2)}, u32[]{:S(2)}) collective-permute-start(f32[16,32,128]{2,1,0:T(8,128)S(1)} %own_second.1.mid), channel_id=1, source_target_pairs={{0,32},{32,0},{64,96},{96,64},{128,160},{160,128},{192,224},{224,1... | collective-permute-start | bytes 786440 | tf_op jit(solution)/shard_map/ppermute | solution.py:287
  84.8 1.4 %collective-permute-done.7.two = f32[16,56,128]{2,1,0:T(8,128)S(1)} collective-permute-done((f32[16,56,128]{2,1,0:T(8,128)S(1)}, f32[16,56,128]{2,1,0:T(8,128)S(1)}, u32[]{:S(2)}, u32[]{:S(2)}) %collective-permute-start.7) | collective-permute-done | bytes 458784 | tf_op jit(solution)/shard_map/ppermute | solution.py:277
  86.2 3.8 %off_second.1.one = f32[16,32,128]{2,1,0:T(8,128)S(1)} custom-call(f32[65,8,128]{2,1,0:T(8,128)S(1)} %collective-permute-done.2.other.msg, f32[16,56,128]{2,1,0:T(8,128)S(1)} %off_first.1.one.mid, f32[16,56,128]{2,1,0:T(8,128)S(1)} %get-tuple-element.16.mid.one, f32[16,56,128]{2,1,0:T(8,128)S(1)} %collective-permute-done.7.two, ...), custom_call_target="tpu_custom_call" | custom-call | flops 4000000000 | bytes 1024 | tf_op jit(solution)/shard_map/off_second/pallas_call | solution.py:213
  90.0 0.8 blend.1
  (13 shorter events, 0.0 us)
Async XLA Ops:
  0.0 0.7 copy-start.3
  0.9 17.9 %copy-start = (f32[32,2048]{1,0:T(8,128)S(1)}, f32[32,2048]{1,0:T(8,128)}, u32[]{:S(2)}) copy-start(f32[32,2048]{1,0:T(8,128)} %mobility.3) | copy-start | bytes 786436
  0.9 17.9 %copy-start.1 = (f32[32,2048]{1,0:T(8,128)S(1)}, f32[32,2048]{1,0:T(8,128)}, u32[]{:S(2)}) copy-start(f32[32,2048]{1,0:T(8,128)} %tilt.3) | copy-start | bytes 786436
  1.9 23.2 %collective-permute-start.2 = (f32[65,8,128]{2,1,0:T(8,128)S(1)}, f32[65,8,128]{2,1,0:T(8,128)S(1)}, u32[]{:S(2)}, u32[]{:S(2)}) collective-permute-start(f32[65,8,128]{2,1,0:T(8,128)S(1)} %pad_maximum_fusion.msg), channel_id=1, source_target_pairs={{0,480},{32,64},{64,32},{96,128},{128,96},{160,192},{192,160},{224... | collective-permute-start | bytes 798728 | tf_op jit(solution)/shard_map/ppermute | solution.py:257
  18.9 41.6 %collective-permute-start = (f32[3,48,8,128]{3,2,1,0:T(8,128)S(1)}, f32[3,48,8,128]{3,2,1,0:T(8,128)S(1)}, u32[]{:S(2)}, u32[]{:S(2)}) collective-permute-start(f32[3,48,8,128]{3,2,1,0:T(8,128)S(1)} %get-tuple-element.13), channel_id=1, source_target_pairs={{1,0},{2,1},{3,2},{4,3},{5,4},{6,5},{7,6},{8,7},{9,8},{10,9},{11,1... | collective-permute-start | bytes 1769480 | tf_op jit(solution)/shard_map/ppermute | solution.py:261
  22.8 37.7 %copy-start.2 = (f32[2048]{0:T(1024)S(1)}, f32[2048]{0:T(1024)}, u32[]{:S(2)}) copy-start(f32[2048]{0:T(1024)} %param.8) | copy-start | bytes 24580
  22.8 37.7 %collective-permute-start.1 = (f32[3,48,8,128]{3,2,1,0:T(8,128)S(1)}, f32[3,48,8,128]{3,2,1,0:T(8,128)S(1)}, u32[]{:S(2)}, u32[]{:S(2)}) collective-permute-start(f32[3,48,8,128]{3,2,1,0:T(8,128)S(1)} %get-tuple-element.14), channel_id=1, source_target_pairs={{0,1},{1,2},{2,3},{3,4},{4,5},{5,6},{6,7},{7,8},{8,9},{9,10},{10,1... | collective-permute-start | bytes 1769480 | tf_op jit(solution)/shard_map/ppermute | solution.py:262
  25.2 35.3 %collective-permute-start.3 = (f32[48,8,128]{2,1,0:T(8,128)S(1)}, f32[48,8,128]{2,1,0:T(8,128)S(1)}, u32[]{:S(2)}, u32[]{:S(2)}) collective-permute-start(f32[48,8,128]{2,1,0:T(8,128)S(1)} %get-tuple-element.15), channel_id=1, source_target_pairs={{0,511},{31,480},{32,95},{63,64},{64,63},{95,32},{96,159},{127,128... | collective-permute-start | bytes 589832 | tf_op jit(solution)/shard_map/ppermute | solution.py:266
  47.7 23.0 %collective-permute-start.4 = (f32[48,8,128]{2,1,0:T(8,128)S(1)}, f32[48,8,128]{2,1,0:T(8,128)S(1)}, u32[]{:S(2)}, u32[]{:S(2)}) collective-permute-start(f32[48,8,128]{2,1,0:T(8,128)S(1)} %get-tuple-element.17), channel_id=1, source_target_pairs={{1,0},{2,1},{3,2},{4,3},{5,4},{6,5},{7,6},{8,7},{9,8},{10,9},{11,1... | collective-permute-start | bytes 589832 | tf_op jit(solution)/shard_map/ppermute | solution.py:264
  49.6 21.1 %collective-permute-start.5 = (f32[48,8,128]{2,1,0:T(8,128)S(1)}, f32[48,8,128]{2,1,0:T(8,128)S(1)}, u32[]{:S(2)}, u32[]{:S(2)}) collective-permute-start(f32[48,8,128]{2,1,0:T(8,128)S(1)} %get-tuple-element.18), channel_id=1, source_target_pairs={{0,1},{1,2},{2,3},{3,4},{4,5},{5,6},{6,7},{7,8},{8,9},{9,10},{10,1... | collective-permute-start | bytes 589832 | tf_op jit(solution)/shard_map/ppermute | solution.py:265
  66.1 11.9 %collective-permute-start.6 = (f32[16,56,128]{2,1,0:T(8,128)S(1)}, f32[16,56,128]{2,1,0:T(8,128)S(1)}, u32[]{:S(2)}, u32[]{:S(2)}) collective-permute-start(f32[16,56,128]{2,1,0:T(8,128)S(1)} %get-tuple-element.16.mid.one), channel_id=1, source_target_pairs={{0,32},{32,0},{64,96},{96,64},{128,160},{160,128},{192,224},{224,1... | collective-permute-start | bytes 1376264 | tf_op jit(solution)/shard_map/ppermute | solution.py:275
  76.1 10.1 %collective-permute-start.7 = (f32[16,56,128]{2,1,0:T(8,128)S(1)}, f32[16,56,128]{2,1,0:T(8,128)S(1)}, u32[]{:S(2)}, u32[]{:S(2)}) collective-permute-start(f32[16,56,128]{2,1,0:T(8,128)S(1)} %off_first.1.one.mid), channel_id=1, source_target_pairs={{0,416},{32,128},{64,480},{96,192},{128,32},{160,256},{192,96},{22... | collective-permute-start | bytes 1376264 | tf_op jit(solution)/shard_map/ppermute | solution.py:277
  81.8 8.2 %collective-permute-start.8 = (f32[16,32,128]{2,1,0:T(8,128)S(1)}, f32[16,32,128]{2,1,0:T(8,128)S(1)}, u32[]{:S(2)}, u32[]{:S(2)}) collective-permute-start(f32[16,32,128]{2,1,0:T(8,128)S(1)} %own_second.1.mid), channel_id=1, source_target_pairs={{0,32},{32,0},{64,96},{96,64},{128,160},{160,128},{192,224},{224,1... | collective-permute-start | bytes 786440 | tf_op jit(solution)/shard_map/ppermute | solution.py:287

commit v4 on v3

--- a/solution.py
+++ b/solution.py
@@ -11,6 +11,7 @@
 RIM = 2 * DEPTH
 LANES = 128
 SUB = 8
+GROUP = 4
 FIRST = 36
 
 
@@ -23,24 +24,25 @@
     lane = lax.broadcasted_iota(jnp.int32, (SUB, LANES), 1)
     is_first = lane == 0
     is_last = lane == LANES - 1
-    for j in range(planes):
-        u = jnp.broadcast_to(drift[j : j + 1, :], (SUB, LANES))
-        rising = u > 0
-        speed = jnp.abs(u)
-        left = (j - 1) % planes
-        right = (j + 1) % planes
+    for begin in range(0, planes, GROUP):
+        group = range(begin, begin + GROUP)
+        drifts = [jnp.broadcast_to(drift[j : j + 1, :], (SUB, LANES)) for j in group]
+        rising = [u > 0 for u in drifts]
+        speed = [jnp.abs(u) for u in drifts]
         for i in range(*span):
             r = i * SUB
-            f = src[j, r : r + SUB, :]
-            below = src[j, r - 1 : r - 1 + SUB, :]
-            above = src[j, r + 1 : r + 1 + SUB, :]
-            west = pltpu.roll(jnp.where(is_last, src[left, r : r + SUB, :], f), 1, 1)
-            east = pltpu.roll(jnp.where(is_first, src[right, r : r + SUB, :], f), LANES - 1, 1)
-            near = (west + east) + (below + above)
-            m = mob[j, r : r + SUB, :]
-            t = tilt[j, r : r + SUB, :]
-            gain = m * ((near + t) - f * (f * f + 3.0))
-            dst[j, r : r + SUB, :] = (f + gain) + speed * (jnp.where(rising, below, above) - f)
+            fields = [src[(begin - 1 + n) % planes, r : r + SUB, :] for n in range(GROUP + 2)]
+            for n, j in enumerate(group):
+                f = fields[n + 1]
+                below = src[j, r - 1 : r - 1 + SUB, :]
+                above = src[j, r + 1 : r + 1 + SUB, :]
+                west = pltpu.roll(jnp.where(is_last, fields[n], f), 1, 1)
+                east = pltpu.roll(jnp.where(is_first, fields[n + 2], f), LANES - 1, 1)
+                near = (west + east) + (below + above)
+                m = mob[j, r : r + SUB, :]
+                t = tilt[j, r : r + SUB, :]
+                gain = m * ((near + t) - f * (f * f + 3.0))
+                dst[j, r : r + SUB, :] = (f + gain) + speed[n] * (jnp.where(rising[n], below, above) - f)
 
 
 def run_cycle(a, b, mob, tilt, drift, begin, end):
@@ -83,7 +85,9 @@
         ref[j, rows - 16 : rows, :] = jnp.zeros((16, LANES), jnp.float32)
 
 
-def edges_kernel(msg, mobility, tilt, down, up):
+def edges_kernel(msg, mobility, tilt, one, two):
+    odd = lax.axis_index("space") % 2 == 1
+    even = lax.axis_index("ladder") % 2 == 0
     planes = mobility.shape[1] // LANES
     tiles = mobility.shape[0] // SUB
     count = RIM // SUB
@@ -94,32 +98,30 @@
             lanes = slice(j * LANES, (j + 1) * LANES)
             lo = slice(i * SUB, (i + 1) * SUB)
             hi = slice((i + skip) * SUB, (i + skip + 1) * SUB)
-            up[0, k] = msg[k + skip * planes]
-            up[1, k] = mobility[hi, lanes]
-            up[2, k] = tilt[hi, lanes]
-            down[0, k] = msg[k]
-            down[1, k] = mobility[lo, lanes]
-            down[2, k] = tilt[lo, lanes]
-
-
-def off_edges_kernel(msg, other, down, up, ends):
-    slab = lax.axis_index("space")
-    low_end = slab == 0
-    high_end = slab == lax.axis_size("space") - 1
-    count = up.shape[0]
+            tops = msg[k + skip * planes], jnp.where(even, mobility[hi, lanes], tilt[hi, lanes])
+            bottoms = msg[k], jnp.where(even, mobility[lo, lanes], tilt[lo, lanes])
+            for n in range(2):
+                one[n, k] = jnp.where(odd, tops[n], bottoms[n])
+                two[n, k] = jnp.where(odd, bottoms[n], tops[n])
+
+
+def off_edges_kernel(other, one, two):
+    odd = lax.axis_index("space") % 2 == 1
+    count = one.shape[0]
     skip = other.shape[0] - 1 - count
     for k in range(count):
         top = other[k + skip]
         bottom = other[k]
-        up[k] = jnp.where(high_end, msg[k + skip], top)
-        down[k] = jnp.where(low_end, msg[k], bottom)
-        ends[k] = jnp.where(low_end, bottom, top)
-
-
-def own_kernel(msg, hi, lo, ends, mobility, tilt, drift, p, mob, til, a, b):
+        one[k] = jnp.where(odd, top, bottom)
+        two[k] = jnp.where(odd, bottom, top)
+
+
+def own_kernel(msg, one, two, on_one, on_two, off_one, mobility, tilt, drift, p, mob, til, a, b):
     slab = lax.axis_index("space")
     low_end = slab == 0
     high_end = slab == lax.axis_size("space") - 1
+    even = lax.axis_index("ladder") % 2 == 0
+    odd = slab % 2 == 1
     height = mobility.shape[0]
     planes = a.shape[0]
     count = RIM // SUB
@@ -128,11 +130,15 @@
     for j in range(planes):
         for i in range(count):
             k = i * planes + j
-            for at, got, alone in ((FIRST - RIM, lo, low_end), (FIRST + height, hi, high_end)):
+            got = [(one[n, k], two[n, k]) for n in range(2)] + [(on_one[k], on_two[k])]
+            lo = [jnp.where(odd, y, x) for x, y in got]
+            hi = [jnp.where(odd, x, y) for x, y in got]
+            for at, g, alone in ((FIRST - RIM, lo, low_end), (FIRST + height, hi, high_end)):
                 rows = slice(at + i * SUB, at + (i + 1) * SUB)
-                a[j, rows, :] = jnp.where(alone, ends[k], got[0, k])
-                mob[j, rows, :] = 0.1 * got[1, k]
-                til[j, rows, :] = got[2, k]
+                a[j, rows, :] = jnp.where(alone, off_one[k], g[0])
+                straight = even != alone
+                mob[j, rows, :] = 0.1 * jnp.where(straight, g[1], g[2])
+                til[j, rows, :] = jnp.where(straight, g[2], g[1])
         for i in range(height // SUB):
             at = FIRST + i * SUB
             rows = slice(i * SUB, (i + 1) * SUB)
@@ -144,15 +150,24 @@
     p[...] = a[:, FIRST - DEPTH : FIRST + height + DEPTH, :]
 
 
-def off_kernel(msg, hi, lo, mob, til, drift, p, a, b):
+def off_kernel(msg, own_one, one, two, mob, til, drift, p, a, b):
+    slab = lax.axis_index("space")
+    low_end = slab == 0
+    high_end = slab == lax.axis_size("space") - 1
+    odd = slab % 2 == 1
     planes = a.shape[0]
     tiles = msg.shape[0] // planes
     height = tiles * SUB
     for ref in (a, b):
         blank(ref)
-    place(a, FIRST - RIM, lo, 0, RIM // SUB)
+    for j in range(planes):
+        for i in range(RIM // SUB):
+            k = i * planes + j
+            r = FIRST - RIM + i * SUB
+            a[j, r : r + SUB, :] = jnp.where(low_end, own_one[0, k], jnp.where(odd, two[k], one[k]))
+            r = FIRST + height + i * SUB
+            a[j, r : r + SUB, :] = jnp.where(high_end, own_one[0, k], jnp.where(odd, one[k], two[k]))
     place(a, FIRST, msg, 0, tiles)
-    place(a, FIRST + height, hi, 0, RIM // SUB)
     run_cycle(a, b, mob, til, drift, FIRST - RIM, FIRST + height + RIM)
     p[...] = a[:, FIRST - DEPTH : FIRST + height + DEPTH, :]
 
@@ -242,13 +257,13 @@
     swap_on = [(i, i ^ 1) for i in range(ladder)]
     swap_beyond = [(i, beyond(i)) for i in range(ladder)]
     both = ("ladder", "space")
-    rise = [
-        (i * space + s, i * space + s + 1 if s < space - 1 else off(i) * space)
+    steps = [
+        (i * space + s, i * space + s + 1 if s < space - 1 else off(i) * space, s)
         for i in range(ladder)
         for s in range(space)
     ]
-    fall = [(b, a) for a, b in rise]
-    at_ends = [(i * space + s, off(i) * space + space - 1 - s) for i in range(ladder) for s in (0, space - 1)]
+    pairs_one = [q for a, b, s in steps if s % 2 == 1 for q in ((a, b), (b, a))]
+    pairs_two = [q for a, b, s in steps if s % 2 == 0 for q in ((a, b), (b, a))]
 
     half = SUB // 2
     tiles = initial.reshape(height // SUB, SUB, planes, LANES).transpose(0, 2, 1, 3).reshape(-1, SUB, LANES)
@@ -257,23 +272,25 @@
     other = lax.ppermute(msg, "ladder", swap_off)
     flow = drift.reshape(planes, LANES)
 
-    down, up = call(edges_kernel, "edges", (msg, mobility, tilt), [(3, *rim)] * 2)
-    own_hi = lax.ppermute(down, both, fall)
-    own_lo = lax.ppermute(up, both, rise)
-    down, up, ends = call(off_edges_kernel, "off_edges", (msg, other), [rim] * 3, ops=4 * 10**10)
-    hi = lax.ppermute(down, both, fall)
-    lo = lax.ppermute(up, both, rise)
-    ends = lax.ppermute(ends, both, at_ends)
+    one, two = call(edges_kernel, "edges", (msg, mobility, tilt), [(2, *rim)] * 2)
+    own_one = lax.ppermute(one, both, pairs_one)
+    own_two = lax.ppermute(two, both, pairs_two)
+    one, two = call(off_edges_kernel, "off_edges", (other,), [rim] * 2, ops=4 * 10**10)
+    one = lax.ppermute(one, both, pairs_one)
+    two = lax.ppermute(two, both, pairs_two)
+    one, two = lax.optimization_barrier((one, two))
+    on_one = lax.ppermute(own_one[1], "ladder", swap_on)
+    on_two = lax.ppermute(own_two[1], "ladder", swap_on)
     p_own, mob, til = call(
         own_kernel,
         "own_first",
-        (msg, own_hi, own_lo, ends, mobility, tilt, flow),
+        (msg, own_one, own_two, on_one, on_two, one, mobility, tilt, flow),
         [wide, work, work],
         [work, work],
         5 * 10**9,
     )
     p_on = lax.ppermute(p_own, "ladder", swap_on)
-    p_off = call(off_kernel, "off_first", (other, hi, lo, mob, til, flow), [wide], [work, work], 5 * 10**9)
+    p_off = call(off_kernel, "off_first", (other, own_one, one, two, mob, til, flow), [wide], [work, work], 5 * 10**9)
     p_beyond = lax.ppermute(p_off, "ladder", swap_beyond)
 
     q_own = call(

time: 91.2 us -> 87.4 us (0.958)
  waiting for transfers between devices: 9.35 us -> 5.59 us
    ppermute x5 -> x6, waiting for transfers between devices: 7.55 us -> 3.95 us  [the longest x1 2.56 us: body(): own_one = lax.ppermute(one, both, pairs_one)]
    ppermute x5 -> x6, starting transfers between devices: 33.6 us -> 37.1 us  [the longest x1 22.3 us: body(): one = lax.ppermute(one, both, pairs_one)]
    ppermute x1, starting transfers between devices: 4.59 us -> 2.05 us  [body(): p_on = lax.ppermute(p_own, 'ladder', swap_on)]
    pallas_call x7, Pallas kernels: 19.5 us -> 18.6 us  [call(): pl.pallas_call(kernel, out_shape=out[0] if single else out, in_specs=[VME...]
  transfers between devices with their start and end apart: 9 -> 10, of which waited for: 3 -> 3; matrix products, arithmetic and copies ran while one was open for 0% -> 0% of each run, Pallas kernels for 21% -> 14%
where the time goes in v4:
time: 87.4 us; the launch traced here: 87 us
  starting transfers between devices  60.7 us (69%)
  Pallas kernels  18.6 us (21%)
  waiting for transfers between devices  5.59 us (6%)
  other arithmetic  1.03 us (1%)
  local copies, waits for them, and re-layouts  0.92 us (1%)
    ppermute x1, starting transfers between devices, body(): one = lax.ppermute(one, both, pairs_one)  22.3 us
    pallas_call x7, Pallas kernels, call(): pl.pallas_call(kernel, out_shape=out[0] if single else out, in_specs=[VME...  18.6 us
    ppermute x1, starting transfers between devices, body(): other = lax.ppermute(msg, 'ladder', swap_off)  16.8 us
    ppermute x1, starting transfers between devices, body(): on_one = lax.ppermute(own_one[1], 'ladder', swap_on)  4.5 us
    ppermute x1, starting transfers between devices, body(): own_one = lax.ppermute(one, both, pairs_one)  3.91 us
    ppermute x1, starting transfers between devices, body(): q_on = lax.ppermute(q_own, 'ladder', swap_on)  2.85 us
    ppermute x1, waiting for transfers between devices, body(): own_one = lax.ppermute(one, both, pairs_one)  2.56 us
    ppermute x1, starting transfers between devices, body(): own_two = lax.ppermute(two, both, pairs_two)  2.5 us
  transfers between devices with their start and end apart: 10, of which 3 were waited for; matrix products, arithmetic and copies ran while one was open for 0% of the time, Pallas kernels for 14%

profile of v4, /device:TPU:1, one launch (start us, length us, event | category | flops | bytes accessed | tf_op | source)
XLA Modules:
  0.0 87.0 jit_solution(5743081190186901532)
XLA Ops:
  0.0 0.7 copy-done.3
  0.7 0.1 broadcast_in_dim.15
  0.7 0.1 broadcast_in_dim.16
  0.8 0.1 broadcast_in_dim.17
  0.9 1.0 %pad_maximum_fusion.msg = f32[65,8,128]{2,1,0:T(8,128)S(1)} fusion(f32[1,8,128]{2,1,0:T(8,128)S(1)} %broadcast_in_dim.17, f32[64,8,128]{2,1,0:T(8,128)} %bitcast.16), kind=kLoop, calls=%fused_computation | loop fusion | flops 66560 | bytes 532480 | tf_op jit(solution)/shard_map/concatenate | solution.py:271
  1.9 16.8 %collective-permute-start.4 = (f32[65,8,128]{2,1,0:T(8,128)S(1)}, f32[65,8,128]{2,1,0:T(8,128)S(1)}, u32[]{:S(2)}, u32[]{:S(2)}) collective-permute-start(f32[65,8,128]{2,1,0:T(8,128)S(1)} %pad_maximum_fusion.msg), channel_id=1, source_target_pairs={{0,480},{32,64},{64,32},{96,128},{128,96},{160,192},{192,160},{224... | collective-permute-start | bytes 798728 | tf_op jit(solution)/shard_map/ppermute | solution.py:272
  18.8 0.1 edges.1
  18.9 3.9 %collective-permute-start = (f32[2,48,8,128]{3,2,1,0:T(8,128)S(1)}, f32[2,48,8,128]{3,2,1,0:T(8,128)S(1)}, u32[]{:S(2)}, u32[]{:S(2)}) collective-permute-start(f32[2,48,8,128]{3,2,1,0:T(8,128)S(1)} %get-tuple-element.14), channel_id=1, source_target_pairs={{1,2},{2,1},{3,4},{4,3},{5,6},{6,5},{7,8},{8,7},{9,10},{10,9},{11,... | collective-permute-start | bytes 1179656 | tf_op jit(solution)/shard_map/ppermute | solution.py:276
  22.8 2.5 %collective-permute-start.1 = (f32[2,48,8,128]{3,2,1,0:T(8,128)S(1)}, f32[2,48,8,128]{3,2,1,0:T(8,128)S(1)}, u32[]{:S(2)}, u32[]{:S(2)}) collective-permute-start(f32[2,48,8,128]{3,2,1,0:T(8,128)S(1)} %get-tuple-element.15), channel_id=1, source_target_pairs={{0,1},{1,0},{2,3},{3,2},{4,5},{5,4},{6,7},{7,6},{8,9},{9,8},{10,11... | collective-permute-start | bytes 1179656 | tf_op jit(solution)/shard_map/ppermute | solution.py:277
  25.3 22.3 %collective-permute-start.5 = (f32[48,8,128]{2,1,0:T(8,128)S(1)}, f32[48,8,128]{2,1,0:T(8,128)S(1)}, u32[]{:S(2)}, u32[]{:S(2)}) collective-permute-start(f32[48,8,128]{2,1,0:T(8,128)S(1)} %get-tuple-element.16), channel_id=1, source_target_pairs={{1,2},{2,1},{3,4},{4,3},{5,6},{6,5},{7,8},{8,7},{9,10},{10,9},{11,... | collective-permute-start | bytes 589832 | tf_op jit(solution)/shard_map/ppermute | solution.py:279
  47.7 1.9 %collective-permute-start.6 = (f32[48,8,128]{2,1,0:T(8,128)S(1)}, f32[48,8,128]{2,1,0:T(8,128)S(1)}, u32[]{:S(2)}, u32[]{:S(2)}) collective-permute-start(f32[48,8,128]{2,1,0:T(8,128)S(1)} %get-tuple-element.17), channel_id=1, source_target_pairs={{0,1},{1,0},{2,3},{3,2},{4,5},{5,4},{6,7},{7,6},{8,9},{9,8},{10,11... | collective-permute-start | bytes 589832 | tf_op jit(solution)/shard_map/ppermute | solution.py:280
  49.6 2.6 %collective-permute-done.one.own_one = f32[2,48,8,128]{3,2,1,0:T(8,128)S(1)} collective-permute-done((f32[2,48,8,128]{3,2,1,0:T(8,128)S(1)}, f32[2,48,8,128]{3,2,1,0:T(8,128)S(1)}, u32[]{:S(2)}, u32[]{:S(2)}) %collective-permute-start) | collective-permute-done | bytes 393248 | tf_op jit(solution)/shard_map/ppermute | solution.py:276
  52.2 4.5 %collective-permute-start.2 = (f32[48,8,128]{2,1,0:T(8,128)S(1)}, f32[48,8,128]{2,1,0:T(8,128)S(1)}, u32[]{:S(2)}, u32[]{:S(2)}) collective-permute-start(f32[48,8,128]{2,1,0:T(8,128)S(1)} %slice_bitcast_fusion.1), channel_id=1, source_target_pairs={{0,32},{32,0},{64,96},{96,64},{128,160},{160,128},{192,224},{224,1... | collective-permute-start | bytes 589832 | tf_op jit(solution)/shard_map/ppermute | solution.py:282
  56.7 1.9 %collective-permute-start.3 = (f32[48,8,128]{2,1,0:T(8,128)S(1)}, f32[48,8,128]{2,1,0:T(8,128)S(1)}, u32[]{:S(2)}, u32[]{:S(2)}) collective-permute-start(f32[48,8,128]{2,1,0:T(8,128)S(1)} %slice_bitcast_fusion), channel_id=1, source_target_pairs={{0,32},{32,0},{64,96},{96,64},{128,160},{160,128},{192,224},{224,1... | collective-permute-start | bytes 589832 | tf_op jit(solution)/shard_map/ppermute | solution.py:283
  58.7 1.4 %collective-permute-done.3.on_two = f32[48,8,128]{2,1,0:T(8,128)S(1)} collective-permute-done((f32[48,8,128]{2,1,0:T(8,128)S(1)}, f32[48,8,128]{2,1,0:T(8,128)S(1)}, u32[]{:S(2)}, u32[]{:S(2)}) %collective-permute-start.3) | collective-permute-done | bytes 196640 | tf_op jit(solution)/shard_map/ppermute | solution.py:283
  60.1 5.3 %own_first.1 = (f32[16,56,128]{2,1,0:T(8,128)S(1)}, f32[16,104,128]{2,1,0:T(8,128)S(1)}, f32[16,104,128]{2,1,0:T(8,128)S(1)}) custom-call(f32[65,8,128]{2,1,0:T(8,128)S(1)} %pad_maximum_fusion.msg, f32[2,48,8,128]{3,2,1,0:T(8,128)S(1)} %collective-permute-done.one.own_one, f32[2,48,8,128]{3,2,1,0:T(8,128)S(1)} %collective-permute-done.1.two, ...), custom_call_target="tpu_custom_call" | custom-call | flops 5000000000 | bytes 1024 | tf_op jit(solution)/shard_map/own_first/pallas_call | solution.py:228
  65.3 2.0 %collective-permute-start.7 = (f32[16,56,128]{2,1,0:T(8,128)S(1)}, f32[16,56,128]{2,1,0:T(8,128)S(1)}, u32[]{:S(2)}, u32[]{:S(2)}) collective-permute-start(f32[16,56,128]{2,1,0:T(8,128)S(1)} %get-tuple-element.19.mid.one), channel_id=1, source_target_pairs={{0,32},{32,0},{64,96},{96,64},{128,160},{160,128},{192,224},{224,1... | collective-permute-start | bytes 1376264 | tf_op jit(solution)/shard_map/ppermute | solution.py:292
  67.4 5.1 %off_first.1.one.mid = f32[16,56,128]{2,1,0:T(8,128)S(1)} custom-call(f32[65,8,128]{2,1,0:T(8,128)S(1)} %collective-permute-done.4.other.msg, f32[2,48,8,128]{3,2,1,0:T(8,128)S(1)} %collective-permute-done.one.own_one, f32[48,8,128]{2,1,0:T(8,128)S(1)} %collective-permute-done.5.off_one.one, f32[48,8,128]{2,1,0:T(8,128)S(1)} %collective-permute-done.6.two, ...), custom_call_target="tpu_custom_call" | custom-call | flops 5000000000 | bytes 1024 | tf_op jit(solution)/shard_map/off_first/pallas_call | solution.py:228
  72.5 1.9 %collective-permute-start.8 = (f32[16,56,128]{2,1,0:T(8,128)S(1)}, f32[16,56,128]{2,1,0:T(8,128)S(1)}, u32[]{:S(2)}, u32[]{:S(2)}) collective-permute-start(f32[16,56,128]{2,1,0:T(8,128)S(1)} %off_first.1.one.mid), channel_id=1, source_target_pairs={{0,416},{32,128},{64,480},{96,192},{128,32},{160,256},{192,96},{22... | collective-permute-start | bytes 1376264 | tf_op jit(solution)/shard_map/ppermute | solution.py:294
  74.4 3.7 %own_second.1.mid = f32[16,32,128]{2,1,0:T(8,128)S(1)} custom-call(f32[65,8,128]{2,1,0:T(8,128)S(1)} %pad_maximum_fusion.msg, f32[16,56,128]{2,1,0:T(8,128)S(1)} %get-tuple-element.19.mid.one, f32[16,56,128]{2,1,0:T(8,128)S(1)} %off_first.1.one.mid, f32[16,56,128]{2,1,0:T(8,128)S(1)} %collective-permute-done.7.two, ...), custom_call_target="tpu_custom_call" | custom-call | flops 4000000000 | bytes 1024 | tf_op jit(solution)/shard_map/own_second/pallas_call | solution.py:228
  78.1 2.8 %collective-permute-start.9 = (f32[16,32,128]{2,1,0:T(8,128)S(1)}, f32[16,32,128]{2,1,0:T(8,128)S(1)}, u32[]{:S(2)}, u32[]{:S(2)}) collective-permute-start(f32[16,32,128]{2,1,0:T(8,128)S(1)} %own_second.1.mid), channel_id=1, source_target_pairs={{0,32},{32,0},{64,96},{96,64},{128,160},{160,128},{192,224},{224,1... | collective-permute-start | bytes 786440 | tf_op jit(solution)/shard_map/ppermute | solution.py:304
  80.9 1.6 %collective-permute-done.8.two = f32[16,56,128]{2,1,0:T(8,128)S(1)} collective-permute-done((f32[16,56,128]{2,1,0:T(8,128)S(1)}, f32[16,56,128]{2,1,0:T(8,128)S(1)}, u32[]{:S(2)}, u32[]{:S(2)}) %collective-permute-start.8) | collective-permute-done | bytes 458784 | tf_op jit(solution)/shard_map/ppermute | solution.py:294
  82.6 3.7 %off_second.1.one = f32[16,32,128]{2,1,0:T(8,128)S(1)} custom-call(f32[65,8,128]{2,1,0:T(8,128)S(1)} %collective-permute-done.4.other.msg, f32[16,56,128]{2,1,0:T(8,128)S(1)} %off_first.1.one.mid, f32[16,56,128]{2,1,0:T(8,128)S(1)} %get-tuple-element.19.mid.one, f32[16,56,128]{2,1,0:T(8,128)S(1)} %collective-permute-done.8.two, ...), custom_call_target="tpu_custom_call" | custom-call | flops 4000000000 | bytes 1024 | tf_op jit(solution)/shard_map/off_second/pallas_call | solution.py:228
  86.2 0.8 blend.1
  (17 shorter events, 0.1 us)
Async XLA Ops:
  0.0 0.7 copy-start.3
  0.9 17.9 %copy-start = (f32[32,2048]{1,0:T(8,128)S(1)}, f32[32,2048]{1,0:T(8,128)}, u32[]{:S(2)}) copy-start(f32[32,2048]{1,0:T(8,128)} %mobility.3) | copy-start | bytes 786436
  0.9 17.9 %copy-start.1 = (f32[32,2048]{1,0:T(8,128)S(1)}, f32[32,2048]{1,0:T(8,128)}, u32[]{:S(2)}) copy-start(f32[32,2048]{1,0:T(8,128)} %tilt.3) | copy-start | bytes 786436
  1.9 23.4 %collective-permute-start.4 = (f32[65,8,128]{2,1,0:T(8,128)S(1)}, f32[65,8,128]{2,1,0:T(8,128)S(1)}, u32[]{:S(2)}, u32[]{:S(2)}) collective-permute-start(f32[65,8,128]{2,1,0:T(8,128)S(1)} %pad_maximum_fusion.msg), channel_id=1, source_target_pairs={{0,480},{32,64},{64,32},{96,128},{128,96},{160,192},{192,160},{224... | collective-permute-start | bytes 798728 | tf_op jit(solution)/shard_map/ppermute | solution.py:272
  18.9 33.3 %collective-permute-start = (f32[2,48,8,128]{3,2,1,0:T(8,128)S(1)}, f32[2,48,8,128]{3,2,1,0:T(8,128)S(1)}, u32[]{:S(2)}, u32[]{:S(2)}) collective-permute-start(f32[2,48,8,128]{3,2,1,0:T(8,128)S(1)} %get-tuple-element.14), channel_id=1, source_target_pairs={{1,2},{2,1},{3,4},{4,3},{5,6},{6,5},{7,8},{8,7},{9,10},{10,9},{11,... | collective-permute-start | bytes 1179656 | tf_op jit(solution)/shard_map/ppermute | solution.py:276
  22.8 33.9 %collective-permute-start.1 = (f32[2,48,8,128]{3,2,1,0:T(8,128)S(1)}, f32[2,48,8,128]{3,2,1,0:T(8,128)S(1)}, u32[]{:S(2)}, u32[]{:S(2)}) collective-permute-start(f32[2,48,8,128]{3,2,1,0:T(8,128)S(1)} %get-tuple-element.15), channel_id=1, source_target_pairs={{0,1},{1,0},{2,3},{3,2},{4,5},{5,4},{6,7},{7,6},{8,9},{9,8},{10,11... | collective-permute-start | bytes 1179656 | tf_op jit(solution)/shard_map/ppermute | solution.py:277
  25.3 33.3 %collective-permute-start.5 = (f32[48,8,128]{2,1,0:T(8,128)S(1)}, f32[48,8,128]{2,1,0:T(8,128)S(1)}, u32[]{:S(2)}, u32[]{:S(2)}) collective-permute-start(f32[48,8,128]{2,1,0:T(8,128)S(1)} %get-tuple-element.16), channel_id=1, source_target_pairs={{1,2},{2,1},{3,4},{4,3},{5,6},{6,5},{7,8},{8,7},{9,10},{10,9},{11,... | collective-permute-start | bytes 589832 | tf_op jit(solution)/shard_map/ppermute | solution.py:279
  47.7 11.0 %collective-permute-start.6 = (f32[48,8,128]{2,1,0:T(8,128)S(1)}, f32[48,8,128]{2,1,0:T(8,128)S(1)}, u32[]{:S(2)}, u32[]{:S(2)}) collective-permute-start(f32[48,8,128]{2,1,0:T(8,128)S(1)} %get-tuple-element.17), channel_id=1, source_target_pairs={{0,1},{1,0},{2,3},{3,2},{4,5},{5,4},{6,7},{7,6},{8,9},{9,8},{10,11... | collective-permute-start | bytes 589832 | tf_op jit(solution)/shard_map/ppermute | solution.py:280
  52.2 7.9 %copy-start.2 = (f32[2048]{0:T(1024)S(1)}, f32[2048]{0:T(1024)}, u32[]{:S(2)}) copy-start(f32[2048]{0:T(1024)} %param.8) | copy-start | bytes 24580
  52.2 6.5 %collective-permute-start.2 = (f32[48,8,128]{2,1,0:T(8,128)S(1)}, f32[48,8,128]{2,1,0:T(8,128)S(1)}, u32[]{:S(2)}, u32[]{:S(2)}) collective-permute-start(f32[48,8,128]{2,1,0:T(8,128)S(1)} %slice_bitcast_fusion.1), channel_id=1, source_target_pairs={{0,32},{32,0},{64,96},{96,64},{128,160},{160,128},{192,224},{224,1... | collective-permute-start | bytes 589832 | tf_op jit(solution)/shard_map/ppermute | solution.py:282
  56.7 3.3 %collective-permute-start.3 = (f32[48,8,128]{2,1,0:T(8,128)S(1)}, f32[48,8,128]{2,1,0:T(8,128)S(1)}, u32[]{:S(2)}, u32[]{:S(2)}) collective-permute-start(f32[48,8,128]{2,1,0:T(8,128)S(1)} %slice_bitcast_fusion), channel_id=1, source_target_pairs={{0,32},{32,0},{64,96},{96,64},{128,160},{160,128},{192,224},{224,1... | collective-permute-start | bytes 589832 | tf_op jit(solution)/shard_map/ppermute | solution.py:283
  65.3 9.1 %collective-permute-start.7 = (f32[16,56,128]{2,1,0:T(8,128)S(1)}, f32[16,56,128]{2,1,0:T(8,128)S(1)}, u32[]{:S(2)}, u32[]{:S(2)}) collective-permute-start(f32[16,56,128]{2,1,0:T(8,128)S(1)} %get-tuple-element.19.mid.one), channel_id=1, source_target_pairs={{0,32},{32,0},{64,96},{96,64},{128,160},{160,128},{192,224},{224,1... | collective-permute-start | bytes 1376264 | tf_op jit(solution)/shard_map/ppermute | solution.py:292
  72.5 10.1 %collective-permute-start.8 = (f32[16,56,128]{2,1,0:T(8,128)S(1)}, f32[16,56,128]{2,1,0:T(8,128)S(1)}, u32[]{:S(2)}, u32[]{:S(2)}) collective-permute-start(f32[16,56,128]{2,1,0:T(8,128)S(1)} %off_first.1.one.mid), channel_id=1, source_target_pairs={{0,416},{32,128},{64,480},{96,192},{128,32},{160,256},{192,96},{22... | collective-permute-start | bytes 1376264 | tf_op jit(solution)/shard_map/ppermute | solution.py:294
  78.1 8.2 %collective-permute-start.9 = (f32[16,32,128]{2,1,0:T(8,128)S(1)}, f32[16,32,128]{2,1,0:T(8,128)S(1)}, u32[]{:S(2)}, u32[]{:S(2)}) collective-permute-start(f32[16,32,128]{2,1,0:T(8,128)S(1)} %own_second.1.mid), channel_id=1, source_target_pairs={{0,32},{32,0},{64,96},{96,64},{128,160},{160,128},{192,224},{224,1... | collective-permute-start | bytes 786440 | tf_op jit(solution)/shard_map/ppermute | solution.py:304

commit v5 on v4

--- a/solution.py
+++ b/solution.py
@@ -85,6 +85,18 @@
         ref[j, rows - 16 : rows, :] = jnp.zeros((16, LANES), jnp.float32)
 
 
+def pack_kernel(field, pair, msg):
+    planes = field.shape[1] // LANES
+    half = SUB // 2
+    for i in range(field.shape[0] // SUB):
+        for j in range(planes):
+            msg[i * planes + j] = field[i * SUB : (i + 1) * SUB, j * LANES : (j + 1) * LANES]
+    lower = jnp.broadcast_to(pair[0:1, 0:1], (SUB, LANES))
+    upper = jnp.broadcast_to(pair[0:1, 1:2], (SUB, LANES))
+    row = lax.broadcasted_iota(jnp.int32, (SUB, LANES), 0)
+    msg[msg.shape[0] - 1] = jnp.where(row < half, lower, upper)
+
+
 def edges_kernel(msg, mobility, tilt, one, two):
     odd = lax.axis_index("space") % 2 == 1
     even = lax.axis_index("ladder") % 2 == 0
@@ -265,10 +277,7 @@
     pairs_one = [q for a, b, s in steps if s % 2 == 1 for q in ((a, b), (b, a))]
     pairs_two = [q for a, b, s in steps if s % 2 == 0 for q in ((a, b), (b, a))]
 
-    half = SUB // 2
-    tiles = initial.reshape(height // SUB, SUB, planes, LANES).transpose(0, 2, 1, 3).reshape(-1, SUB, LANES)
-    pair = jnp.broadcast_to(mix_weights.reshape(2, 1, 1), (2, half, LANES)).reshape(1, SUB, LANES)
-    msg = jnp.concatenate([tiles, pair])
+    msg = call(pack_kernel, "pack", (initial[0], mix_weights), [(planes * height // SUB + 1, SUB, LANES)])
     other = lax.ppermute(msg, "ladder", swap_off)
     flow = drift.reshape(planes, LANES)
 

time: 87.4 us -> 87.3 us (level)
  other arithmetic: 1.03 us -> 0 us
    concatenate x1 -> x0, other arithmetic: 1.03 us -> none  [body(): msg = jnp.concatenate([tiles, pair])]
    unnamed x8 -> x10, local copies, waits for them, and re-layouts: 0.67 us -> 1.62 us
    pallas_call x7 -> x8, Pallas kernels: 18.6 us -> 18.6 us  [call(): pl.pallas_call(kernel, out_shape=out[0] if single else out, in_specs=[VME...]
where the time goes in v5:
time: 87.3 us; the launch traced here: 86.9 us
  starting transfers between devices  60.8 us (70%)
  Pallas kernels  18.6 us (21%)
  waiting for transfers between devices  5.59 us (6%)
  local copies, waits for them, and re-layouts  1.65 us (2%)
    ppermute x1, starting transfers between devices, body(): one = lax.ppermute(one, both, pairs_one)  22.3 us
    pallas_call x8, Pallas kernels, call(): pl.pallas_call(kernel, out_shape=out[0] if single else out, in_specs=[VME...  18.6 us
    ppermute x1, starting transfers between devices, body(): other = lax.ppermute(msg, 'ladder', swap_off)  17 us
    ppermute x1, starting transfers between devices, body(): on_one = lax.ppermute(own_one[1], 'ladder', swap_on)  4.5 us
    ppermute x1, starting transfers between devices, body(): own_one = lax.ppermute(one, both, pairs_one)  3.91 us
    ppermute x1, starting transfers between devices, body(): q_on = lax.ppermute(q_own, 'ladder', swap_on)  2.85 us
    ppermute x1, waiting for transfers between devices, body(): own_one = lax.ppermute(one, both, pairs_one)  2.56 us
    ppermute x1, starting transfers between devices, body(): own_two = lax.ppermute(two, both, pairs_two)  2.5 us
  transfers between devices with their start and end apart: 10, of which 3 were waited for; matrix products, arithmetic and copies ran while one was open for 0% of the time, Pallas kernels for 14%

profile of v5, /device:TPU:1, one launch (start us, length us, event | category | flops | bytes accessed | tf_op | source)
XLA Modules:
  0.0 86.9 jit_solution(6017073082647050667)
XLA Ops:
  0.0 0.7 copy-done.3
  0.7 0.9 %copy-done.2 = f32[1,32,2048]{2,1,0:T(8,128)S(1)} copy-done((f32[1,32,2048]{2,1,0:T(8,128)S(1)}, f32[1,32,2048]{2,1,0:T(8,128)}, u32[]{:S(2)}) %copy-start.2) | copy-done | bytes 262168
  1.6 0.1 pack.1.msg
  1.7 17.0 %collective-permute-start.4 = (f32[65,8,128]{2,1,0:T(8,128)S(1)}, f32[65,8,128]{2,1,0:T(8,128)S(1)}, u32[]{:S(2)}, u32[]{:S(2)}) collective-permute-start(f32[65,8,128]{2,1,0:T(8,128)S(1)} %pack.1.msg), channel_id=1, source_target_pairs={{0,480},{32,64},{64,32},{96,128},{128,96},{160,192},{192,160},{224... | collective-permute-start | bytes 798728 | tf_op jit(solution)/shard_map/ppermute | solution.py:281
  18.7 0.1 edges.1
  18.7 3.9 %collective-permute-start = (f32[2,48,8,128]{3,2,1,0:T(8,128)S(1)}, f32[2,48,8,128]{3,2,1,0:T(8,128)S(1)}, u32[]{:S(2)}, u32[]{:S(2)}) collective-permute-start(f32[2,48,8,128]{3,2,1,0:T(8,128)S(1)} %get-tuple-element.14), channel_id=1, source_target_pairs={{1,2},{2,1},{3,4},{4,3},{5,6},{6,5},{7,8},{8,7},{9,10},{10,9},{11,... | collective-permute-start | bytes 1179656 | tf_op jit(solution)/shard_map/ppermute | solution.py:285
  22.7 2.5 %collective-permute-start.1 = (f32[2,48,8,128]{3,2,1,0:T(8,128)S(1)}, f32[2,48,8,128]{3,2,1,0:T(8,128)S(1)}, u32[]{:S(2)}, u32[]{:S(2)}) collective-permute-start(f32[2,48,8,128]{3,2,1,0:T(8,128)S(1)} %get-tuple-element.15), channel_id=1, source_target_pairs={{0,1},{1,0},{2,3},{3,2},{4,5},{5,4},{6,7},{7,6},{8,9},{9,8},{10,11... | collective-permute-start | bytes 1179656 | tf_op jit(solution)/shard_map/ppermute | solution.py:286
  25.2 22.3 %collective-permute-start.5 = (f32[48,8,128]{2,1,0:T(8,128)S(1)}, f32[48,8,128]{2,1,0:T(8,128)S(1)}, u32[]{:S(2)}, u32[]{:S(2)}) collective-permute-start(f32[48,8,128]{2,1,0:T(8,128)S(1)} %get-tuple-element.16), channel_id=1, source_target_pairs={{1,2},{2,1},{3,4},{4,3},{5,6},{6,5},{7,8},{8,7},{9,10},{10,9},{11,... | collective-permute-start | bytes 589832 | tf_op jit(solution)/shard_map/ppermute | solution.py:288
  47.5 1.9 %collective-permute-start.6 = (f32[48,8,128]{2,1,0:T(8,128)S(1)}, f32[48,8,128]{2,1,0:T(8,128)S(1)}, u32[]{:S(2)}, u32[]{:S(2)}) collective-permute-start(f32[48,8,128]{2,1,0:T(8,128)S(1)} %get-tuple-element.17), channel_id=1, source_target_pairs={{0,1},{1,0},{2,3},{3,2},{4,5},{5,4},{6,7},{7,6},{8,9},{9,8},{10,11... | collective-permute-start | bytes 589832 | tf_op jit(solution)/shard_map/ppermute | solution.py:289
  49.5 2.6 %collective-permute-done.one.own_one = f32[2,48,8,128]{3,2,1,0:T(8,128)S(1)} collective-permute-done((f32[2,48,8,128]{3,2,1,0:T(8,128)S(1)}, f32[2,48,8,128]{3,2,1,0:T(8,128)S(1)}, u32[]{:S(2)}, u32[]{:S(2)}) %collective-permute-start) | collective-permute-done | bytes 393248 | tf_op jit(solution)/shard_map/ppermute | solution.py:285
  52.1 0.0 copy-start.4
  52.1 4.5 %collective-permute-start.2 = (f32[48,8,128]{2,1,0:T(8,128)S(1)}, f32[48,8,128]{2,1,0:T(8,128)S(1)}, u32[]{:S(2)}, u32[]{:S(2)}) collective-permute-start(f32[48,8,128]{2,1,0:T(8,128)S(1)} %slice_bitcast_fusion.1), channel_id=1, source_target_pairs={{0,32},{32,0},{64,96},{96,64},{128,160},{160,128},{192,224},{224,1... | collective-permute-start | bytes 589832 | tf_op jit(solution)/shard_map/ppermute | solution.py:291
  56.6 0.0 collective-permute-done.1.two
  56.6 1.9 %collective-permute-start.3 = (f32[48,8,128]{2,1,0:T(8,128)S(1)}, f32[48,8,128]{2,1,0:T(8,128)S(1)}, u32[]{:S(2)}, u32[]{:S(2)}) collective-permute-start(f32[48,8,128]{2,1,0:T(8,128)S(1)} %slice_bitcast_fusion), channel_id=1, source_target_pairs={{0,32},{32,0},{64,96},{96,64},{128,160},{160,128},{192,224},{224,1... | collective-permute-start | bytes 589832 | tf_op jit(solution)/shard_map/ppermute | solution.py:292
  58.6 1.4 %collective-permute-done.3.on_two = f32[48,8,128]{2,1,0:T(8,128)S(1)} collective-permute-done((f32[48,8,128]{2,1,0:T(8,128)S(1)}, f32[48,8,128]{2,1,0:T(8,128)S(1)}, u32[]{:S(2)}, u32[]{:S(2)}) %collective-permute-start.3) | collective-permute-done | bytes 196640 | tf_op jit(solution)/shard_map/ppermute | solution.py:292
  59.9 5.3 %own_first.1 = (f32[16,56,128]{2,1,0:T(8,128)S(1)}, f32[16,104,128]{2,1,0:T(8,128)S(1)}, f32[16,104,128]{2,1,0:T(8,128)S(1)}) custom-call(f32[65,8,128]{2,1,0:T(8,128)S(1)} %pack.1.msg, f32[2,48,8,128]{3,2,1,0:T(8,128)S(1)} %collective-permute-done.one.own_one, f32[2,48,8,128]{3,2,1,0:T(8,128)S(1)} %collective-permute-done.1.two, ...), custom_call_target="tpu_custom_call" | custom-call | flops 5000000000 | bytes 1024 | tf_op jit(solution)/shard_map/own_first/pallas_call | solution.py:240
  65.2 2.0 %collective-permute-start.7 = (f32[16,56,128]{2,1,0:T(8,128)S(1)}, f32[16,56,128]{2,1,0:T(8,128)S(1)}, u32[]{:S(2)}, u32[]{:S(2)}) collective-permute-start(f32[16,56,128]{2,1,0:T(8,128)S(1)} %get-tuple-element.19.mid.one), channel_id=1, source_target_pairs={{0,32},{32,0},{64,96},{96,64},{128,160},{160,128},{192,224},{224,1... | collective-permute-start | bytes 1376264 | tf_op jit(solution)/shard_map/ppermute | solution.py:301
  67.3 5.1 %off_first.1.one.mid = f32[16,56,128]{2,1,0:T(8,128)S(1)} custom-call(f32[65,8,128]{2,1,0:T(8,128)S(1)} %collective-permute-done.4.other.msg, f32[2,48,8,128]{3,2,1,0:T(8,128)S(1)} %collective-permute-done.one.own_one, f32[48,8,128]{2,1,0:T(8,128)S(1)} %collective-permute-done.5.off_one.one, f32[48,8,128]{2,1,0:T(8,128)S(1)} %collective-permute-done.6.two, ...), custom_call_target="tpu_custom_call" | custom-call | flops 5000000000 | bytes 1024 | tf_op jit(solution)/shard_map/off_first/pallas_call | solution.py:240
  72.4 1.9 %collective-permute-start.8 = (f32[16,56,128]{2,1,0:T(8,128)S(1)}, f32[16,56,128]{2,1,0:T(8,128)S(1)}, u32[]{:S(2)}, u32[]{:S(2)}) collective-permute-start(f32[16,56,128]{2,1,0:T(8,128)S(1)} %off_first.1.one.mid), channel_id=1, source_target_pairs={{0,416},{32,128},{64,480},{96,192},{128,32},{160,256},{192,96},{22... | collective-permute-start | bytes 1376264 | tf_op jit(solution)/shard_map/ppermute | solution.py:303
  74.3 3.7 %own_second.1.mid = f32[16,32,128]{2,1,0:T(8,128)S(1)} custom-call(f32[65,8,128]{2,1,0:T(8,128)S(1)} %pack.1.msg, f32[16,56,128]{2,1,0:T(8,128)S(1)} %get-tuple-element.19.mid.one, f32[16,56,128]{2,1,0:T(8,128)S(1)} %off_first.1.one.mid, f32[16,56,128]{2,1,0:T(8,128)S(1)} %collective-permute-done.7.two, f32[16,104,128]{2,1,0:T(8,128)S(1)} %get-tuple-element.21.mob, ...), custom_call_target="tpu_custom_call" | custom-call | flops 4000000000 | bytes 1024 | tf_op jit(solution)/shard_map/own_second/pallas_call | solution.py:240
  78.0 2.8 %collective-permute-start.9 = (f32[16,32,128]{2,1,0:T(8,128)S(1)}, f32[16,32,128]{2,1,0:T(8,128)S(1)}, u32[]{:S(2)}, u32[]{:S(2)}) collective-permute-start(f32[16,32,128]{2,1,0:T(8,128)S(1)} %own_second.1.mid), channel_id=1, source_target_pairs={{0,32},{32,0},{64,96},{96,64},{128,160},{160,128},{192,224},{224,1... | collective-permute-start | bytes 786440 | tf_op jit(solution)/shard_map/ppermute | solution.py:313
  80.8 1.6 %collective-permute-done.8.two = f32[16,56,128]{2,1,0:T(8,128)S(1)} collective-permute-done((f32[16,56,128]{2,1,0:T(8,128)S(1)}, f32[16,56,128]{2,1,0:T(8,128)S(1)}, u32[]{:S(2)}, u32[]{:S(2)}) %collective-permute-start.8) | collective-permute-done | bytes 458784 | tf_op jit(solution)/shard_map/ppermute | solution.py:303
  82.4 3.7 %off_second.1.one = f32[16,32,128]{2,1,0:T(8,128)S(1)} custom-call(f32[65,8,128]{2,1,0:T(8,128)S(1)} %collective-permute-done.4.other.msg, f32[16,56,128]{2,1,0:T(8,128)S(1)} %off_first.1.one.mid, f32[16,56,128]{2,1,0:T(8,128)S(1)} %get-tuple-element.19.mid.one, f32[16,56,128]{2,1,0:T(8,128)S(1)} %collective-permute-done.8.two, ...), custom_call_target="tpu_custom_call" | custom-call | flops 4000000000 | bytes 1024 | tf_op jit(solution)/shard_map/off_second/pallas_call | solution.py:240
  86.1 0.8 blend.1
  (16 shorter events, 0.1 us)
Async XLA Ops:
  0.0 0.7 copy-start.3
  0.7 0.9 %copy-start.2 = (f32[1,32,2048]{2,1,0:T(8,128)S(1)}, f32[1,32,2048]{2,1,0:T(8,128)}, u32[]{:S(2)}) copy-start(f32[1,32,2048]{2,1,0:T(8,128)} %param.5) | copy-start | bytes 786436
  1.6 17.0 %copy-start = (f32[32,2048]{1,0:T(8,128)S(1)}, f32[32,2048]{1,0:T(8,128)}, u32[]{:S(2)}) copy-start(f32[32,2048]{1,0:T(8,128)} %mobility.3) | copy-start | bytes 786436
  1.6 17.0 %copy-start.1 = (f32[32,2048]{1,0:T(8,128)S(1)}, f32[32,2048]{1,0:T(8,128)}, u32[]{:S(2)}) copy-start(f32[32,2048]{1,0:T(8,128)} %tilt.3) | copy-start | bytes 786436
  1.7 23.5 %collective-permute-start.4 = (f32[65,8,128]{2,1,0:T(8,128)S(1)}, f32[65,8,128]{2,1,0:T(8,128)S(1)}, u32[]{:S(2)}, u32[]{:S(2)}) collective-permute-start(f32[65,8,128]{2,1,0:T(8,128)S(1)} %pack.1.msg), channel_id=1, source_target_pairs={{0,480},{32,64},{64,32},{96,128},{128,96},{160,192},{192,160},{224... | collective-permute-start | bytes 798728 | tf_op jit(solution)/shard_map/ppermute | solution.py:281
  18.7 33.3 %collective-permute-start = (f32[2,48,8,128]{3,2,1,0:T(8,128)S(1)}, f32[2,48,8,128]{3,2,1,0:T(8,128)S(1)}, u32[]{:S(2)}, u32[]{:S(2)}) collective-permute-start(f32[2,48,8,128]{3,2,1,0:T(8,128)S(1)} %get-tuple-element.14), channel_id=1, source_target_pairs={{1,2},{2,1},{3,4},{4,3},{5,6},{6,5},{7,8},{8,7},{9,10},{10,9},{11,... | collective-permute-start | bytes 1179656 | tf_op jit(solution)/shard_map/ppermute | solution.py:285
  22.7 33.9 %collective-permute-start.1 = (f32[2,48,8,128]{3,2,1,0:T(8,128)S(1)}, f32[2,48,8,128]{3,2,1,0:T(8,128)S(1)}, u32[]{:S(2)}, u32[]{:S(2)}) collective-permute-start(f32[2,48,8,128]{3,2,1,0:T(8,128)S(1)} %get-tuple-element.15), channel_id=1, source_target_pairs={{0,1},{1,0},{2,3},{3,2},{4,5},{5,4},{6,7},{7,6},{8,9},{9,8},{10,11... | collective-permute-start | bytes 1179656 | tf_op jit(solution)/shard_map/ppermute | solution.py:286
  25.2 33.3 %collective-permute-start.5 = (f32[48,8,128]{2,1,0:T(8,128)S(1)}, f32[48,8,128]{2,1,0:T(8,128)S(1)}, u32[]{:S(2)}, u32[]{:S(2)}) collective-permute-start(f32[48,8,128]{2,1,0:T(8,128)S(1)} %get-tuple-element.16), channel_id=1, source_target_pairs={{1,2},{2,1},{3,4},{4,3},{5,6},{6,5},{7,8},{8,7},{9,10},{10,9},{11,... | collective-permute-start | bytes 589832 | tf_op jit(solution)/shard_map/ppermute | solution.py:288
  47.5 11.0 %collective-permute-start.6 = (f32[48,8,128]{2,1,0:T(8,128)S(1)}, f32[48,8,128]{2,1,0:T(8,128)S(1)}, u32[]{:S(2)}, u32[]{:S(2)}) collective-permute-start(f32[48,8,128]{2,1,0:T(8,128)S(1)} %get-tuple-element.17), channel_id=1, source_target_pairs={{0,1},{1,0},{2,3},{3,2},{4,5},{5,4},{6,7},{7,6},{8,9},{9,8},{10,11... | collective-permute-start | bytes 589832 | tf_op jit(solution)/shard_map/ppermute | solution.py:289
  52.1 7.9 %copy-start.4 = (f32[2048]{0:T(1024)S(1)}, f32[2048]{0:T(1024)}, u32[]{:S(2)}) copy-start(f32[2048]{0:T(1024)} %param.8) | copy-start | bytes 24580
  52.1 6.5 %collective-permute-start.2 = (f32[48,8,128]{2,1,0:T(8,128)S(1)}, f32[48,8,128]{2,1,0:T(8,128)S(1)}, u32[]{:S(2)}, u32[]{:S(2)}) collective-permute-start(f32[48,8,128]{2,1,0:T(8,128)S(1)} %slice_bitcast_fusion.1), channel_id=1, source_target_pairs={{0,32},{32,0},{64,96},{96,64},{128,160},{160,128},{192,224},{224,1... | collective-permute-start | bytes 589832 | tf_op jit(solution)/shard_map/ppermute | solution.py:291
  56.6 3.3 %collective-permute-start.3 = (f32[48,8,128]{2,1,0:T(8,128)S(1)}, f32[48,8,128]{2,1,0:T(8,128)S(1)}, u32[]{:S(2)}, u32[]{:S(2)}) collective-permute-start(f32[48,8,128]{2,1,0:T(8,128)S(1)} %slice_bitcast_fusion), channel_id=1, source_target_pairs={{0,32},{32,0},{64,96},{96,64},{128,160},{160,128},{192,224},{224,1... | collective-permute-start | bytes 589832 | tf_op jit(solution)/shard_map/ppermute | solution.py:292
  65.2 9.1 %collective-permute-start.7 = (f32[16,56,128]{2,1,0:T(8,128)S(1)}, f32[16,56,128]{2,1,0:T(8,128)S(1)}, u32[]{:S(2)}, u32[]{:S(2)}) collective-permute-start(f32[16,56,128]{2,1,0:T(8,128)S(1)} %get-tuple-element.19.mid.one), channel_id=1, source_target_pairs={{0,32},{32,0},{64,96},{96,64},{128,160},{160,128},{192,224},{224,1... | collective-permute-start | bytes 1376264 | tf_op jit(solution)/shard_map/ppermute | solution.py:301
  72.4 10.1 %collective-permute-start.8 = (f32[16,56,128]{2,1,0:T(8,128)S(1)}, f32[16,56,128]{2,1,0:T(8,128)S(1)}, u32[]{:S(2)}, u32[]{:S(2)}) collective-permute-start(f32[16,56,128]{2,1,0:T(8,128)S(1)} %off_first.1.one.mid), channel_id=1, source_target_pairs={{0,416},{32,128},{64,480},{96,192},{128,32},{160,256},{192,96},{22... | collective-permute-start | bytes 1376264 | tf_op jit(solution)/shard_map/ppermute | solution.py:303
  78.0 8.2 %collective-permute-start.9 = (f32[16,32,128]{2,1,0:T(8,128)S(1)}, f32[16,32,128]{2,1,0:T(8,128)S(1)}, u32[]{:S(2)}, u32[]{:S(2)}) collective-permute-start(f32[16,32,128]{2,1,0:T(8,128)S(1)} %own_second.1.mid), channel_id=1, source_target_pairs={{0,32},{32,0},{64,96},{96,64},{128,160},{160,128},{192,224},{224,1... | collective-permute-start | bytes 786440 | tf_op jit(solution)/shard_map/ppermute | solution.py:313
